TPU v7x, 32 devices: a whole 2x2x4 slice. The times are simulated.
32 devices in a mesh: seq: 2 (over core), rows: 16 (over z, y, x).
Axes of the slice: x: 2, y: 2, z: 4, core: 2. Of those that a mesh axis runs over, the one named last changes fastest.
Arguments:
- tokens: bfloat16 [48, 1024, 768], P('rows', 'seq'), may hold values from -6 to 6
- segment_ids: int32 [48, 1024], P('rows', 'seq'), may hold values from 0 to 5, never falling along the last dimension, each value on 1 to 512 neighbouring positions
- cotangent: bfloat16 [48, 1024, 768], P('rows', 'seq'), may hold values from -6 to 6
- ln1_gain: bfloat16 [768], P(('seq', 'rows')), may hold values from 0.5 to 1.5
- ln1_bias: bfloat16 [768], P(('seq', 'rows')), may hold values from -1.75 to 1.75
- qkv_weight: bfloat16 [768, 2304], P(('seq', 'rows')), may hold values from -0.21875 to 0.21875
- qv_bias: bfloat16 [1536], P(('seq', 'rows')), may hold values from -0.625 to 0.625
- out_weight: bfloat16 [768, 768], P(('seq', 'rows')), may hold values from -0.875 to 0.875
- out_bias: bfloat16 [768], P(('seq', 'rows')), may hold values from -1.75 to 1.75
- ln2_gain: bfloat16 [768], P(('seq', 'rows')), may hold values from 0.5 to 1.5
- ln2_bias: bfloat16 [768], P(('seq', 'rows')), may hold values from -1.75 to 1.75
- up_weight: bfloat16 [768, 3072], P(('seq', 'rows')), may hold values from -0.21875 to 0.21875
- up_bias: bfloat16 [3072], P(('seq', 'rows')), may hold values from -1.75 to 1.75
- down_weight: bfloat16 [3072, 768], P(('seq', 'rows')), may hold values from -0.109375 to 0.109375
- down_bias: bfloat16 [768], P(('seq', 'rows')), may hold values from -1.75 to 1.75
- avg_qkv: float32 [768, 2304], P(('seq', 'rows')), may hold values from -0.21875 to 0.21875
- avg_out: float32 [768, 768], P(('seq', 'rows')), may hold values from -0.875 to 0.875
- avg_up: float32 [768, 3072], P(('seq', 'rows')), may hold values from -0.21875 to 0.21875
- avg_down: float32 [3072, 768], P(('seq', 'rows')), may hold values from -0.109375 to 0.109375
Outputs:
- out_tokens: bfloat16 [48, 1024, 768], P('rows', 'seq')
- grad_input: float32 [48, 1024, 768], P('rows', 'seq')
- grad_ln1_gain: float32 [768], P(('seq', 'rows'))
- grad_ln1_bias: float32 [768], P(('seq', 'rows'))
- grad_qkv_weight: float32 [768, 2304], P(('seq', 'rows'))
- grad_qv_bias: float32 [1536], P(('seq', 'rows'))
- grad_out_weight: float32 [768, 768], P(('seq', 'rows'))
- grad_out_bias: float32 [768], P(('seq', 'rows'))
- grad_ln2_gain: float32 [768], P(('seq', 'rows'))
- grad_ln2_bias: float32 [768], P(('seq', 'rows'))
- grad_up_weight: float32 [768, 3072], P(('seq', 'rows'))
- grad_up_bias: float32 [3072], P(('seq', 'rows'))
- grad_down_weight: float32 [3072, 768], P(('seq', 'rows'))
- grad_down_bias: float32 [768], P(('seq', 'rows'))
- new_avg_qkv: float32 [768, 2304], P(('seq', 'rows'))
- new_avg_out: float32 [768, 768], P(('seq', 'rows'))
- new_avg_up: float32 [768, 3072], P(('seq', 'rows'))
- new_avg_down: float32 [3072, 768], P(('seq', 'rows'))
Inputs may be any that keep to these rules, and one draw needn't show every extreme that they name: `segment_ids`: along each row the ids never fall and every id from 0 to 5 appears; id 5 marks the padding at the end of the row; each id covers 1 to 512 positions of a row, and some id covers exactly 512 positions.
All inputs are finite; a program needn't handle non-finite values.
Results may differ from a plain program's by a relative error of at most 0.011.
Values may be sent and summed in bfloat16 or wider, within the bound.
No kernel may reach another device: no remote copies, remote signals or barrier semaphores. Data moves between devices by JAX's collectives and lax.ppermute only.
A program may use at most 320 MiB of HBM per device.

v0:
```python
import jax
import jax.numpy as jnp
from jax import lax
from jax.sharding import PartitionSpec as P

HEADS = 12
HEAD_DIM = 64
CLIPS = 6


def layer_norm(value, gain, bias):
    middle = jnp.mean(value, axis=-1, keepdims=True)
    centred = value - middle
    spread = jnp.mean(centred * centred, axis=-1, keepdims=True)
    return centred * lax.rsqrt(spread + 1e-06) * gain + bias


def exact_gelu(value):
    return jax.nn.gelu(value, approximate=False)


def permitted(seg_query, seg_key, pos_query, pos_key):
    same_clip = seg_query[:, :, None] == seg_key[:, None, :]
    open_key = (seg_key != CLIPS - 1)[:, None, :]
    diagonal = (pos_query[:, None] == pos_key[None, :])[None]
    return (same_clip & (open_key | diagonal))[:, :, None, :]


def scores(query_part, key_part):
    return 0.125 * jnp.einsum(
        "rqhe,rkhe->rqhk", query_part, key_part, preferred_element_type=jnp.float32
    )


def exponent(score_vals, allowed):
    return jnp.where(allowed, jnp.exp(jnp.where(allowed, score_vals, 0.0)), 0.0)


def on_device(
    tokens,
    segment_ids,
    cotangent,
    ln1_gain,
    ln1_bias,
    qkv_weight,
    qv_bias,
    out_weight,
    out_bias,
    ln2_gain,
    ln2_bias,
    up_weight,
    up_bias,
    down_weight,
    down_bias,
    avg_qkv,
    avg_out,
    avg_up,
    avg_down,
):
    f32 = jnp.float32
    bf16 = jnp.bfloat16
    rows_here, shard_len, width = tokens.shape
    count_rows = rows_here * shard_len
    own_pos = lax.axis_index("seq") * shard_len + jnp.arange(shard_len, dtype=jnp.int32)
    head_shape = (rows_here, shard_len, HEADS, HEAD_DIM)
    gain_one, bias_one, w_qkv, b_qv, w_out, b_out = (
        lax.all_gather(ln1_gain, ("seq", "rows"), axis=0, tiled=True),
        lax.all_gather(ln1_bias, ("seq", "rows"), axis=0, tiled=True),
        lax.all_gather(qkv_weight, ("seq", "rows"), axis=0, tiled=True),
        lax.all_gather(qv_bias, ("seq", "rows"), axis=0, tiled=True),
        lax.all_gather(out_weight, ("seq", "rows"), axis=0, tiled=True),
        lax.all_gather(out_bias, ("seq", "rows"), axis=0, tiled=True),
    )
    residual = tokens.astype(f32).reshape(count_rows, width)
    normed, norm_one_pull = jax.vjp(
        layer_norm, residual, gain_one.astype(f32), bias_one.astype(f32)
    )
    normed_low = normed.astype(bf16)
    mixed = jnp.dot(normed_low, w_qkv, preferred_element_type=f32)
    bias_qv = b_qv.astype(f32)
    query_heads = (mixed[:, :width] + bias_qv[:width]).astype(bf16).reshape(head_shape)
    key_heads = mixed[:, width : 2 * width].astype(bf16).reshape(head_shape)
    value_heads = (mixed[:, 2 * width :] + bias_qv[width:]).astype(bf16).reshape(head_shape)
    start_state = (jnp.zeros((rows_here, shard_len, HEADS), f32), jnp.zeros(head_shape, f32))
    piece_keys = lax.all_gather(key_heads, "seq", axis=1, tiled=True)
    piece_values = lax.all_gather(value_heads, "seq", axis=1, tiled=True)
    piece_seg = lax.all_gather(segment_ids, "seq", axis=1, tiled=True)
    piece_len = piece_keys.shape[1]
    block_len = min(piece_len, shard_len)

    def forward_advance(turn, state):
        totals, weighted = state
        offset = turn * block_len
        key_block = lax.dynamic_slice_in_dim(piece_keys, offset, block_len, 1)
        value_block = lax.dynamic_slice_in_dim(piece_values, offset, block_len, 1)
        seg_block = lax.dynamic_slice_in_dim(piece_seg, offset, block_len, 1)
        key_pos = offset + jnp.arange(block_len, dtype=jnp.int32)
        allowed = permitted(segment_ids, seg_block, own_pos, key_pos)
        expo = exponent(scores(query_heads, key_block), allowed)
        totals = totals + jnp.sum(expo, axis=-1)
        weighted = weighted + jnp.einsum(
            "rqhk,rkhe->rqhe", expo.astype(bf16), value_block, preferred_element_type=f32
        )
        return (totals, weighted)

    totals, weighted = lax.fori_loop(0, piece_len // block_len, forward_advance, start_state)
    attended = weighted / totals[..., None]
    attn_in = attended.reshape(count_rows, width).astype(bf16)
    middle = residual + jnp.dot(attn_in, w_out, preferred_element_type=f32) + b_out.astype(f32)
    gain_two, bias_two, w_up, b_up, w_down, b_down = (
        lax.all_gather(ln2_gain, ("seq", "rows"), axis=0, tiled=True),
        lax.all_gather(ln2_bias, ("seq", "rows"), axis=0, tiled=True),
        lax.all_gather(up_weight, ("seq", "rows"), axis=0, tiled=True),
        lax.all_gather(up_bias, ("seq", "rows"), axis=0, tiled=True),
        lax.all_gather(down_weight, ("seq", "rows"), axis=0, tiled=True),
        lax.all_gather(down_bias, ("seq", "rows"), axis=0, tiled=True),
    )
    normed_two, norm_two_pull = jax.vjp(
        layer_norm, middle, gain_two.astype(f32), bias_two.astype(f32)
    )
    normed_two_low = normed_two.astype(bf16)
    hidden_pre = jnp.dot(normed_two_low, w_up, preferred_element_type=f32) + b_up.astype(f32)
    hidden, gelu_pull = jax.vjp(exact_gelu, hidden_pre)
    hidden_low = hidden.astype(bf16)
    final = middle + jnp.dot(hidden_low, w_down, preferred_element_type=f32) + b_down.astype(f32)
    out_tokens = final.astype(bf16).reshape(tokens.shape)
    w_up_back, w_down_back = (
        lax.all_gather(up_weight, ("seq", "rows"), axis=0, tiled=True),
        lax.all_gather(down_weight, ("seq", "rows"), axis=0, tiled=True),
    )
    grad_out = cotangent.astype(f32).reshape(count_rows, width)
    grad_low = grad_out.astype(bf16)
    grad_down = jnp.einsum("nf,nd->fd", hidden_low, grad_low, preferred_element_type=f32)
    grad_down_b = jnp.sum(grad_low, axis=0, dtype=f32)
    grad_hidden = jnp.einsum("nd,fd->nf", grad_low, w_down_back, preferred_element_type=f32)
    (grad_pre,) = gelu_pull(grad_hidden)
    grad_pre_low = grad_pre.astype(bf16)
    grad_up = jnp.einsum("nd,nf->df", normed_two_low, grad_pre_low, preferred_element_type=f32)
    grad_up_b = jnp.sum(grad_pre_low, axis=0, dtype=f32)
    grad_normed_two = jnp.einsum("nf,df->nd", grad_pre_low, w_up_back, preferred_element_type=f32)
    grad_mid_norm, grad_gain_two, grad_bias_two = norm_two_pull(grad_normed_two)
    grad_mid = grad_out + grad_mid_norm
    mlp_sums = (
        lax.psum_scatter(grad_gain_two, ("seq", "rows"), scatter_dimension=0, tiled=True),
        lax.psum_scatter(grad_bias_two, ("seq", "rows"), scatter_dimension=0, tiled=True),
        lax.psum_scatter(grad_up, ("seq", "rows"), scatter_dimension=0, tiled=True),
        lax.psum_scatter(grad_up_b, ("seq", "rows"), scatter_dimension=0, tiled=True),
        lax.psum_scatter(grad_down, ("seq", "rows"), scatter_dimension=0, tiled=True),
        lax.psum_scatter(grad_down_b, ("seq", "rows"), scatter_dimension=0, tiled=True),
    )
    w_qkv_back, w_out_back = (
        lax.all_gather(qkv_weight, ("seq", "rows"), axis=0, tiled=True),
        lax.all_gather(out_weight, ("seq", "rows"), axis=0, tiled=True),
    )
    grad_mid_low = grad_mid.astype(bf16)
    grad_wout = jnp.einsum("nd,ne->de", attn_in, grad_mid_low, preferred_element_type=f32)
    grad_bout = jnp.sum(grad_mid_low, axis=0, dtype=f32)
    grad_att = jnp.einsum(
        "ne,de->nd", grad_mid_low, w_out_back, preferred_element_type=f32
    ).reshape(head_shape)
    grad_acc = (grad_att / totals[..., None]).astype(bf16)
    shift_low = (jnp.sum(grad_att * attended, axis=-1) / totals).astype(bf16)
    shift_wide = shift_low.astype(f32)
    query_piece_keys = lax.all_gather(key_heads, "seq", axis=1, tiled=True)
    query_piece_values = lax.all_gather(value_heads, "seq", axis=1, tiled=True)
    query_piece_seg = lax.all_gather(segment_ids, "seq", axis=1, tiled=True)
    piece_len = query_piece_keys.shape[1]
    query_block_len = min(piece_len, shard_len)

    def query_advance(turn, grad_query):
        offset = turn * query_block_len
        key_block = lax.dynamic_slice_in_dim(query_piece_keys, offset, query_block_len, 1)
        value_block = lax.dynamic_slice_in_dim(query_piece_values, offset, query_block_len, 1)
        seg_block = lax.dynamic_slice_in_dim(query_piece_seg, offset, query_block_len, 1)
        key_pos = offset + jnp.arange(query_block_len, dtype=jnp.int32)
        allowed = permitted(segment_ids, seg_block, own_pos, key_pos)
        expo = exponent(scores(query_heads, key_block), allowed)
        inner = jnp.einsum("rqhe,rkhe->rqhk", grad_acc, value_block, preferred_element_type=f32)
        grad_score = (expo * (inner - shift_wide[..., None])).astype(bf16)
        return grad_query + jnp.einsum(
            "rqhk,rkhe->rqhe", grad_score, key_block, preferred_element_type=f32
        )

    grad_query = lax.fori_loop(
        0, piece_len // query_block_len, query_advance, jnp.zeros(head_shape, f32)
    )
    key_start = (jnp.zeros(head_shape, f32), jnp.zeros(head_shape, f32))
    piece_queries = lax.all_gather(query_heads, "seq", axis=1, tiled=True)
    piece_grads = lax.all_gather(grad_acc, "seq", axis=1, tiled=True)
    key_piece_seg = lax.all_gather(segment_ids, "seq", axis=1, tiled=True)
    piece_shift = lax.all_gather(shift_low, "seq", axis=1, tiled=True)
    piece_len = piece_queries.shape[1]
    key_block_len = min(piece_len, shard_len)

    def key_advance(turn, state):
        grad_key, grad_value = state
        offset = turn * key_block_len
        query_block = lax.dynamic_slice_in_dim(piece_queries, offset, key_block_len, 1)
        grad_block = lax.dynamic_slice_in_dim(piece_grads, offset, key_block_len, 1)
        seg_block = lax.dynamic_slice_in_dim(key_piece_seg, offset, key_block_len, 1)
        shift_block = lax.dynamic_slice_in_dim(piece_shift, offset, key_block_len, 1).astype(f32)
        query_pos = offset + jnp.arange(key_block_len, dtype=jnp.int32)
        allowed = permitted(seg_block, segment_ids, query_pos, own_pos)
        expo = exponent(scores(query_block, key_heads), allowed)
        inner = jnp.einsum("rqhe,rkhe->rqhk", grad_block, value_heads, preferred_element_type=f32)
        grad_score = (expo * (inner - shift_block[..., None])).astype(bf16)
        grad_key = grad_key + jnp.einsum(
            "rqhk,rqhe->rkhe", grad_score, query_block, preferred_element_type=f32
        )
        grad_value = grad_value + jnp.einsum(
            "rqhk,rqhe->rkhe", expo.astype(bf16), grad_block, preferred_element_type=f32
        )
        return (grad_key, grad_value)

    grad_key, grad_value = lax.fori_loop(0, piece_len // key_block_len, key_advance, key_start)
    grad_q_low = (0.125 * grad_query).astype(bf16).reshape(count_rows, width)
    grad_k_low = (0.125 * grad_key).astype(bf16).reshape(count_rows, width)
    grad_v_low = grad_value.astype(bf16).reshape(count_rows, width)
    grad_mixed = jnp.concatenate([grad_q_low, grad_k_low, grad_v_low], axis=1)
    grad_wqkv = jnp.einsum("nd,ne->de", normed_low, grad_mixed, preferred_element_type=f32)
    grad_bqv = jnp.concatenate(
        [jnp.sum(grad_q_low, axis=0, dtype=f32), jnp.sum(grad_v_low, axis=0, dtype=f32)], axis=0
    )
    grad_normed = jnp.einsum("ne,de->nd", grad_mixed, w_qkv_back, preferred_element_type=f32)
    grad_res_norm, grad_gain_one, grad_bias_one = norm_one_pull(grad_normed)
    grad_input = (grad_mid + grad_res_norm).reshape(tokens.shape)
    attn_sums = (
        lax.psum_scatter(grad_gain_one, ("seq", "rows"), scatter_dimension=0, tiled=True),
        lax.psum_scatter(grad_bias_one, ("seq", "rows"), scatter_dimension=0, tiled=True),
        lax.psum_scatter(grad_wqkv, ("seq", "rows"), scatter_dimension=0, tiled=True),
        lax.psum_scatter(grad_bqv, ("seq", "rows"), scatter_dimension=0, tiled=True),
        lax.psum_scatter(grad_wout, ("seq", "rows"), scatter_dimension=0, tiled=True),
        lax.psum_scatter(grad_bout, ("seq", "rows"), scatter_dimension=0, tiled=True),
    )
    new_qkv = 0.9 * avg_qkv + 0.1 * qkv_weight.astype(f32)
    new_out = 0.9 * avg_out + 0.1 * out_weight.astype(f32)
    new_up = 0.9 * avg_up + 0.1 * up_weight.astype(f32)
    new_down = 0.9 * avg_down + 0.1 * down_weight.astype(f32)
    return (
        out_tokens,
        grad_input,
        attn_sums[0],
        attn_sums[1],
        attn_sums[2],
        attn_sums[3],
        attn_sums[4],
        attn_sums[5],
        mlp_sums[0],
        mlp_sums[1],
        mlp_sums[2],
        mlp_sums[3],
        mlp_sums[4],
        mlp_sums[5],
        new_qkv,
        new_out,
        new_up,
        new_down,
    )


def solution(mesh):
    placed = (
        P("rows", "seq", None),
        P("rows", "seq"),
        P("rows", "seq", None),
        P(("seq", "rows")),
        P(("seq", "rows")),
        P(("seq", "rows"), None),
        P(("seq", "rows")),
        P(("seq", "rows"), None),
        P(("seq", "rows")),
        P(("seq", "rows")),
        P(("seq", "rows")),
        P(("seq", "rows"), None),
        P(("seq", "rows")),
        P(("seq", "rows"), None),
        P(("seq", "rows")),
        P(("seq", "rows"), None),
        P(("seq", "rows"), None),
        P(("seq", "rows"), None),
        P(("seq", "rows"), None),
    )
    return jax.shard_map(
        on_device,
        mesh=mesh,
        in_specs=placed,
        out_specs=(
            P("rows", "seq", None),
            P("rows", "seq", None),
            P(("seq", "rows")),
            P(("seq", "rows")),
            P(("seq", "rows"), None),
            P(("seq", "rows")),
            P(("seq", "rows"), None),
            P(("seq", "rows")),
            P(("seq", "rows")),
            P(("seq", "rows")),
            P(("seq", "rows"), None),
            P(("seq", "rows")),
            P(("seq", "rows"), None),
            P(("seq", "rows")),
            P(("seq", "rows"), None),
            P(("seq", "rows"), None),
            P(("seq", "rows"), None),
            P(("seq", "rows"), None),
        ),
        check_vma=False,
    )
```

profile of v0, /device:TPU:0, one launch (start us, length us, event | category | flops | bytes accessed | tf_op | source)
XLA Modules:
  0.0 923.5 jit_solution(5376381607204456000)
XLA Ops:
  14.7 42.9 %all-reduce.17 = (bf16[768]{0:T(1024)(128)(2,1)S(1)}, bf16[768]{0:T(1024)(128)(2,1)S(1)}, bf16[1536]{0:T(1024)(128)(2,1)S(1)}, bf16[768]{0:T(1024)(128)(2,1)S(1)...) all-reduce(bf16[768]{0:T(1024)(128)(2,1)S(1)} %dynamic-update-slice, ...), channel_id=1, replica_groups=mesh['seq'=2,'rows'=16] {'seq','rows'}, use_global_device_ids=true, to_apply=%add.1 | all-reduce | flops 9216 | bytes 36864
  59.8 2.5 fusion.92
  62.9 2.3 fusion.88
  65.2 8.6 all-gather.9.cloned.1.call-done
  73.8 8.5 fusion.106
  82.4 5.1 copy-done.14
  87.7 2.4 copy.69
  90.1 6.5 reshape.285
  96.9 6.0 fusion.80
  102.8 2.4 copy.71
  105.3 7.0 reshape.287
  119.9 3.1 copy.70
  123.0 4.1 reshape.286
  127.0 2.7 copy.73
  129.9 6.8 copy.72
  136.7 6.9 copy.74
  143.6 81.4 %while.46 = (s32[]{:T(128)}, f32[3,512,12]{1,2,0:T(8,128)S(1)}, f32[3,512,12,64]{1,3,2,0:T(8,128)}, s32[3,512]{1,0:T(4,128)S(1)}, s32[3,1024]{1,0:T(4,128)S(1)},...) while((s32[]{:T(128)}, f32[3,512,12]{1,2,0:T(8,128)S(1)}, ...), condition=%wide.region_4.5_spmd.clone, body=%wide.region_2.4_spmd.clone.sunk | while | flops 2496418304 | bytes 95227088 | solution.py:106
  144.9 18.8 %fusion.161 = (f32[3,512,12]{1,2,0:T(8,128)S(1)}, f32[3,12,512,512]{3,2,1,0:T(8,128)}) fusion(pred[3,512,512]{1,2,0:T(8,128)(4,1)S(1)} %or_and_fusion.6, bf16[3,512,12,64]{1,3,2,0:T(8,128)(2,1)S(1)} %get-tuple-element.1088, bf16[3,1024,12,64]{1,3,2,0:T(8,128)(2,1)} %get-tuple-element.1087, s32[]{:T(128)S(6)} %select_n.160), kind=kOutput, calls=%fused_computation.7.clone.1 | convolution fusion | flops 1245689856 | bytes 43327492 | tf_op jit(solution)/shard_map/while/body/eval_jaxpr/rqhe,rkhe->rqhk/dot_general | solution.py:30
  163.7 19.8 %bitcast_add_fusion.10 = f32[3,512,12,64]{1,3,2,0:T(8,128)} fusion(f32[3,512,12,64]{1,3,2,0:T(8,128)} %get-tuple-element.1071, pred[]{:T(512)S(6)} %compare.9, f32[3,12,512,512]{3,2,1,0:T(8,128)} %get-tuple-element.1028, pred[3,512,512]{1,2,0:T(8,128)(4,1)S(1)} %or_and_fusion.6, bf16[3,1024,12,64]{1,3,2,0:T(8,128)(2,1)} %get-tuple-element.1089, ...), kind=kOutput, calls=%fused_computation.10.clone.1 | convolution fusion | flops 1248067584 | bytes 50331652 | tf_op jit(solution)/shard_map/while/body/eval_jaxpr/rqhk,rkhe->rqhe/dot_general | solution.py:101
  184.6 18.9 %fusion.161 = (f32[3,512,12]{1,2,0:T(8,128)S(1)}, f32[3,12,512,512]{3,2,1,0:T(8,128)}) fusion(pred[3,512,512]{1,2,0:T(8,128)(4,1)S(1)} %or_and_fusion.6, bf16[3,512,12,64]{1,3,2,0:T(8,128)(2,1)S(1)} %get-tuple-element.1088, bf16[3,1024,12,64]{1,3,2,0:T(8,128)(2,1)} %get-tuple-element.1087, s32[]{:T(128)S(6)} %select_n.160), kind=kOutput, calls=%fused_computation.7.clone.1 | convolution fusion | flops 1245689856 | bytes 43327492 | tf_op jit(solution)/shard_map/while/body/eval_jaxpr/rqhe,rkhe->rqhk/dot_general | solution.py:30
  203.5 21.1 %bitcast_add_fusion.10 = f32[3,512,12,64]{1,3,2,0:T(8,128)} fusion(f32[3,512,12,64]{1,3,2,0:T(8,128)} %get-tuple-element.1071, pred[]{:T(512)S(6)} %compare.9, f32[3,12,512,512]{3,2,1,0:T(8,128)} %get-tuple-element.1028, pred[3,512,512]{1,2,0:T(8,128)(4,1)S(1)} %or_and_fusion.6, bf16[3,1024,12,64]{1,3,2,0:T(8,128)(2,1)} %get-tuple-element.1089, ...), kind=kOutput, calls=%fused_computation.10.clone.1 | convolution fusion | flops 1248067584 | bytes 50331652 | tf_op jit(solution)/shard_map/while/body/eval_jaxpr/rqhk,rkhe->rqhe/dot_general | solution.py:101
  225.1 6.4 fusion.96
  231.5 2.2 copy.96
  233.8 5.2 fusion.105
  242.4 10.6 %all-gather.17.cloned.1.call-done = bf16[768,3072]{1,0:T(8,128)(2,1)} async-done(((bf16[24,3072]{1,0:T(8,128)(2,1)}), bf16[768,3072]{1,0:T(8,128)(2,1)}) %all-gather.17.cloned.1.call-update) | async-done | bytes 4718608 | tf_op jit(solution)/shard_map/all_gather | solution.py:113
  253.0 54.3 %multiply_convert_fusion = (bf16[1536,3072]{1,0:T(8,128)(2,1)}, f32[1536,3072]{1,0:T(8,128)}, f32[1536,3072]{1,0:T(8,128)}) fusion(f32[3072]{0:T(1024)S(1)} %copy-done.52, bf16[768,3072]{1,0:T(8,128)(2,1)} %all-gather.17.cloned.1.call-done, f32[1536,768]{1,0:T(8,128)} %copy-done.11, f32[768]{0:T(1024)S(1)} %copy-done.54, f32[768]{0:T(1024)S(1)} %copy-done.51, ...), kind=kOutput, calls=%fused_computation.85 | convolution fusion | flops 7565082624 | bytes 56653824 | tf_op jit(solution)/shard_map/dot_general | solution.py:122
  307.2 10.9 %all-gather.19.cloned.1.call-done = bf16[3072,768]{1,0:T(8,128)(2,1)} async-done(((bf16[96,768]{1,0:T(8,128)(2,1)}), bf16[3072,768]{1,0:T(8,128)(2,1)}) %all-gather.19.cloned.1.call-update) | async-done | bytes 4718608 | tf_op jit(solution)/shard_map/all_gather | solution.py:115
  318.1 23.9 %convert_reduce_fusion = (f32[3072]{0:T(1024)}, bf16[1536,3072]{1,0:T(8,128)(2,1)}) fusion(f32[1536,3072]{1,0:T(8,128)} %get-tuple-element.826, bf16[1536,768]{1,0:T(8,128)(2,1)S(1)} %copy-done.21, bf16[3072,768]{1,0:T(8,128)(2,1)} %all-gather.19.cloned.1.call-done, f32[1536,3072]{1,0:T(8,128)} %get-tuple-element.843, f32[3072]{0:T(1024)S(1)} %copy-done.52), kind=kOutput, calls=%fused_computation.83 | convolution fusion | flops 7327970304 | bytes 54288384 | tf_op jit(solution)/shard_map/nd,fd->nf/dot_general | solution.py:135
  342.0 13.4 %multiply_reduce_fusion.1 = (f32[768]{0:T(1024)}, f32[1536]{0:T(1024)S(1)}, f32[768]{0:T(1024)}, f32[1536,768]{1,0:T(8,128)S(1)}) fusion(f32[1536,768]{1,0:T(8,128)S(1)} %copy-done.12, f32[1536]{0:T(1024)S(1)} %fusion.95, f32[1536]{0:T(1024)S(1)} %broadcast_multiply_fusion, f32[768]{0:T(1024)S(1)} %copy-done.51, ...), kind=kOutput, calls=%fused_computation.128 | convolution fusion | flops 7257191424 | bytes 23620608 | tf_op jit(solution)/shard_map/nf,df->nd/dot_general | solution.py:140
  355.5 2.2 fusion.102
  361.4 4.2 fusion.107
  365.6 8.5 reshape.290
  374.0 10.5 %multiply_reduce_fusion = (f32[3,512,12]{1,0,2:T(4,128)S(1)}, bf16[3,512,12,64]{1,0,3,2:T(4,128)(2,1)}) fusion(f32[3,512,12,64]{1,0,3,2:T(4,128)} %reshape.290, f32[3,512,12]{1,0,2:T(4,128)S(1)} %copy-done.26, f32[3,512,12,64]{1,3,2,0:T(8,128)} %get-tuple-element.527), kind=kLoop, calls=%fused_computation.102 | loop fusion | flops 5879808 | bytes 11943936 | tf_op jit(solution)/shard_map/reduce_sum | solution.py:162
  384.6 6.0 fusion.109
  392.9 5.6 copy.88
  398.5 2.1 copy.82
  401.4 13.1 %fusion.98 = f32[768,3072]{1,0:T(8,128)} fusion(bf16[1536,3072]{1,0:T(8,128)(2,1)} %get-tuple-element.847, f32[1536,768]{1,0:T(8,128)S(1)} %bitcast.187, f32[768]{0:T(1024)S(1)} %copy-done.54, f32[768]{0:T(1024)S(1)} %copy-done.51, f32[1536]{0:T(1024)S(1)} %fusion.95, f32[1536]{0:T(1024)S(1)} %broadcast_multiply_fusion), kind=kOutput, calls=%fused_computation.160 | convolution fusion | flops 7253655552 | bytes 23611392 | tf_op jit(solution)/shard_map/nd,nf->df/dot_general | solution.py:138
  416.2 83.0 %while.47 = (s32[]{:T(128)}, f32[3,512,12,64]{1,3,2,0:T(8,128)}, bf16[3,1024,12,64]{1,3,2,0:T(8,128)(2,1)}, s32[3,512]{1,0:T(4,128)S(1)}, s32[3,1024]{1,0:T(4,12...) while((s32[]{:T(128)}, f32[3,512,12,64]{1,3,2,0:T(8,128)}, ...), condition=%wide.region_11.12_spmd.clone, body=%wide.region_10.11_spmd.clone.sunk | while | flops 3685485056 | bytes 98939608 | solution.py:184
  416.2 17.0 %fusion.168 = f32[3,12,512,512]{3,2,1,0:T(8,128)} fusion(bf16[3,512,12,64]{1,3,2,0:T(8,128)(2,1)S(1)} %get-tuple-element.1128, bf16[3,1024,12,64]{1,3,2,0:T(8,128)(2,1)} %get-tuple-element.1125, s32[]{:T(128)S(6)} %select_n.163), kind=kOutput, calls=%fused_computation.38.clone.1 | convolution fusion | flops 1207959552 | bytes 42467332 | tf_op jit(solution)/shard_map/while/body/eval_jaxpr/rqhe,rkhe->rqhk/dot_general | solution.py:30
  434.2 23.1 %bitcast_add_fusion.11 = f32[3,512,12,64]{1,3,2,0:T(8,128)} fusion(f32[3,512,12,64]{1,3,2,0:T(8,128)} %get-tuple-element.1110, pred[]{:T(512)S(6)} %compare.10, f32[3,12,512,512]{3,2,1,0:T(8,128)} %fusion.168, f32[3,512,12]{1,2,0:T(8,128)S(1)} %get-tuple-element.1131, pred[3,512,512]{1,2,0:T(8,128)(4,1)S(1)} %or_and_fusion.7, ...), kind=kOutput, calls=%fused_computation.34.clone.1 | convolution fusion | flops 2474901504 | bytes 55125504 | tf_op jit(solution)/shard_map/while/body/eval_jaxpr/rqhk,rkhe->rqhe/dot_general | solution.py:180
  457.4 16.8 %fusion.168 = f32[3,12,512,512]{3,2,1,0:T(8,128)} fusion(bf16[3,512,12,64]{1,3,2,0:T(8,128)(2,1)S(1)} %get-tuple-element.1128, bf16[3,1024,12,64]{1,3,2,0:T(8,128)(2,1)} %get-tuple-element.1125, s32[]{:T(128)S(6)} %select_n.163), kind=kOutput, calls=%fused_computation.38.clone.1 | convolution fusion | flops 1207959552 | bytes 42467332 | tf_op jit(solution)/shard_map/while/body/eval_jaxpr/rqhe,rkhe->rqhk/dot_general | solution.py:30
  475.2 23.9 %bitcast_add_fusion.11 = f32[3,512,12,64]{1,3,2,0:T(8,128)} fusion(f32[3,512,12,64]{1,3,2,0:T(8,128)} %get-tuple-element.1110, pred[]{:T(512)S(6)} %compare.10, f32[3,12,512,512]{3,2,1,0:T(8,128)} %fusion.168, f32[3,512,12]{1,2,0:T(8,128)S(1)} %get-tuple-element.1131, pred[3,512,512]{1,2,0:T(8,128)(4,1)S(1)} %or_and_fusion.7, ...), kind=kOutput, calls=%fused_computation.34.clone.1 | convolution fusion | flops 2474901504 | bytes 55125504 | tf_op jit(solution)/shard_map/while/body/eval_jaxpr/rqhk,rkhe->rqhe/dot_general | solution.py:180
  499.2 3.4 convert_reduce_fusion.5
  505.5 2.2 all_gather.79
  509.3 10.2 %fusion.110 = f32[3072,768]{1,0:T(8,128)} fusion(bf16[1536,3072]{1,0:T(8,128)(2,1)S(1)} %copy-done.60, bf16[1536,768]{1,0:T(8,128)(2,1)S(1)} %copy-done.22), kind=kOutput, calls=%fused_computation.170 | convolution fusion | flops 7247757312 | bytes 21233664 | tf_op jit(solution)/shard_map/nf,nd->fd/dot_general | solution.py:133
  519.6 7.2 copy.85
  526.8 7.2 copy.87
  534.1 127.3 %while.48 = (s32[]{:T(128)}, f32[3,512,12,64]{1,3,2,0:T(8,128)}, f32[3,512,12,64]{1,3,2,0:T(8,128)}, bf16[3,1024,12,64]{1,3,2,0:T(8,128)(2,1)}, s32[3,1024]{1,0:...) while((s32[]{:T(128)}, f32[3,512,12,64]{1,3,2,0:T(8,128)}, ...), condition=%wide.region_13.14_spmd.clone, body=%wide.region_12.13_spmd.clone.sunk | while | flops 4933571072 | bytes 149461744 | solution.py:215
  534.5 18.2 %fusion.176 = f32[3,12,512,512]{3,2,1,0:T(8,128)} fusion(bf16[3,512,12,64]{1,3,2,0:T(8,128)(2,1)S(1)} %get-tuple-element.1173, bf16[3,1024,12,64]{1,3,2,0:T(8,128)(2,1)} %get-tuple-element.1170, s32[]{:T(128)S(6)} %select_n.168), kind=kOutput, calls=%fused_computation.65.clone.1 | convolution fusion | flops 1207959552 | bytes 42467332 | tf_op jit(solution)/shard_map/while/body/eval_jaxpr/rqhe,rkhe->rqhk/dot_general | solution.py:30
  553.9 23.8 %bitcast_add_fusion.12 = f32[3,512,12,64]{1,3,2,0:T(8,128)} fusion(f32[3,512,12,64]{1,3,2,0:T(8,128)} %get-tuple-element.1153, pred[]{:T(512)S(6)} %compare.11, f32[3,12,512,512]{3,2,1,0:T(8,128)} %fusion.176, f32[3,512,12]{1,2,0:T(8,128)S(1)} %copy_convert_fusion.2, pred[3,512,512]{2,1,0:T(8,128)(4,1)S(1)} %or_and_fusion.8, ...), kind=kOutput, calls=%fused_computation.60.clone.1 | convolution fusion | flops 2474901504 | bytes 55125504 | tf_op jit(solution)/shard_map/while/body/eval_jaxpr/rqhk,rqhe->rkhe/dot_general | solution.py:207
  577.6 20.2 %bitcast_add_fusion.13 = f32[3,512,12,64]{1,3,2,0:T(8,128)} fusion(f32[3,512,12,64]{1,3,2,0:T(8,128)} %get-tuple-element.1154, pred[]{:T(512)S(6)} %compare.11, f32[3,12,512,512]{3,2,1,0:T(8,128)} %fusion.176, pred[3,512,512]{2,1,0:T(8,128)(4,1)S(1)} %or_and_fusion.8, bf16[3,1024,12,64]{1,3,2,0:T(8,128)(2,1)} %get-tuple-element.1174, s32[]{:T(128)S(6)} %select_n.168), kind=kOutput, calls=%fused_computation.59.clone.1 | convolution fusion | flops 1248067584 | bytes 50331652 | tf_op jit(solution)/shard_map/while/body/eval_jaxpr/rqhk,rqhe->rkhe/dot_general | solution.py:210
  597.8 17.1 %fusion.176 = f32[3,12,512,512]{3,2,1,0:T(8,128)} fusion(bf16[3,512,12,64]{1,3,2,0:T(8,128)(2,1)S(1)} %get-tuple-element.1173, bf16[3,1024,12,64]{1,3,2,0:T(8,128)(2,1)} %get-tuple-element.1170, s32[]{:T(128)S(6)} %select_n.168), kind=kOutput, calls=%fused_computation.65.clone.1 | convolution fusion | flops 1207959552 | bytes 42467332 | tf_op jit(solution)/shard_map/while/body/eval_jaxpr/rqhe,rkhe->rqhk/dot_general | solution.py:30
  616.1 24.0 %bitcast_add_fusion.12 = f32[3,512,12,64]{1,3,2,0:T(8,128)} fusion(f32[3,512,12,64]{1,3,2,0:T(8,128)} %get-tuple-element.1153, pred[]{:T(512)S(6)} %compare.11, f32[3,12,512,512]{3,2,1,0:T(8,128)} %fusion.176, f32[3,512,12]{1,2,0:T(8,128)S(1)} %copy_convert_fusion.2, pred[3,512,512]{2,1,0:T(8,128)(4,1)S(1)} %or_and_fusion.8, ...), kind=kOutput, calls=%fused_computation.60.clone.1 | convolution fusion | flops 2474901504 | bytes 55125504 | tf_op jit(solution)/shard_map/while/body/eval_jaxpr/rqhk,rqhe->rkhe/dot_general | solution.py:207
  640.1 21.1 %bitcast_add_fusion.13 = f32[3,512,12,64]{1,3,2,0:T(8,128)} fusion(f32[3,512,12,64]{1,3,2,0:T(8,128)} %get-tuple-element.1154, pred[]{:T(512)S(6)} %compare.11, f32[3,12,512,512]{3,2,1,0:T(8,128)} %fusion.176, pred[3,512,512]{2,1,0:T(8,128)(4,1)S(1)} %or_and_fusion.8, bf16[3,1024,12,64]{1,3,2,0:T(8,128)(2,1)} %get-tuple-element.1174, s32[]{:T(128)S(6)} %select_n.168), kind=kOutput, calls=%fused_computation.59.clone.1 | convolution fusion | flops 1248067584 | bytes 50331652 | tf_op jit(solution)/shard_map/while/body/eval_jaxpr/rqhk,rqhe->rkhe/dot_general | solution.py:210
  661.4 5.2 convert_reduce_fusion.4
  672.6 3.1 copy-done.27
  675.8 7.9 fusion.108
  689.8 14.0 %add_convert_fusion.1 = bf16[1536,768]{1,0:T(8,128)(2,1)} fusion(f32[1536,768]{1,0:T(8,128)} %copy-done.11, bf16[1536,3072]{1,0:T(8,128)(2,1)} %get-tuple-element.825, bf16[3072,768]{1,0:T(8,128)(2,1)} %all-gather.19.cloned.1.call-done, f32[768]{0:T(1024)S(1)} %convert_element_type.161), kind=kOutput, calls=%fused_computation.136 | convolution fusion | flops 7251296256 | bytes 21236736 | tf_op jit(solution)/shard_map/dot_general | solution.py:125
  704.0 9.9 %fusion.100 = (f32[768]{0:T(1024)S(1)}, f32[1536]{0:T(1024)S(1)}, f32[1536,768]{1,0:T(8,128)S(1)}) fusion(f32[768]{0:T(1024)S(1)} %copy-done.48, f32[1536]{0:T(1024)S(1)} %copy-done.37, bf16[3,512,768]{2,1,0:T(8,128)(2,1)S(1)} %copy-done.4, bf16[1536,2304]{0,1:T(8,128)(2,1)} %copy-done.27, bf16[768,2304]{1,0:T(8,128)(2,1)} %all-gather.9.cloned.1.call-done), kind=kOutput, calls=%fused_computation.162 | convolution fusion | flops 5442893312 | bytes 17713152 | tf_op jit(solution)/shard_map/ne,de->nd/dot_general | solution.py:224
  716.1 2.6 fusion.89
  718.7 41.3 %all-reduce.16 = (f32[768]{0:T(1024)S(1)}, f32[768]{0:T(1024)S(1)}, f32[1536]{0:T(1024)S(1)}, f32[768]{0:T(1024)S(1)}, f32[768]{0:T(1024)S(1)}, /*index=5*/f32[7...) all-reduce(f32[768]{0:T(1024)S(1)} %get-tuple-element.732, ...), channel_id=2, replica_groups=mesh['seq'=2,'rows'=16] {'seq','rows'}, use_global_device_ids=true, to_apply=%region_17.18.clone | all-reduce | flops 9216 | bytes 73728
  764.7 8.2 add_add_fusion.2
  772.9 18.2 %reduce-scatter.11.cloned.1.call-done = f32[96,768]{1,0:T(8,128)} async-done(((f32[3072,768]{1,0:T(8,128)}), f32[96,768]{1,0:T(8,128)}) %reduce-scatter.11.cloned.1.call-update) | async-done | bytes 294928 | tf_op jit(solution)/shard_map/reduce_scatter | solution.py:148
  791.1 125.4 %reduce-scatter.5.cloned.1.call-done = f32[24,2304]{1,0:T(8,128)} async-done(((f32[768,2304]{1,0:T(8,128)}), f32[24,2304]{1,0:T(8,128)}) %reduce-scatter.5.cloned.1.call-update) | async-done | bytes 221200 | tf_op jit(solution)/shard_map/reduce_scatter | solution.py:230
  (268 shorter events, 60.0 us)
Async XLA Ops:
  7.2 55.7 %copy-start.3 = (bf16[3,512,768]{2,1,0:T(8,128)(2,1)S(1)}, bf16[3,512,768]{2,1,0:T(8,128)(2,1)}, u32[]{:S(2)}) copy-start(bf16[3,512,768]{2,1,0:T(8,128)(2,1)} %param.25) | copy-start | bytes 7077892
  7.2 66.6 %all-gather.9.cloned.1.call-start = ((), (), s32[]{:S(2)}) async-start(), calls=%async_computation.4 | async-start | bytes 3649536 | tf_op jit(solution)/shard_map/all_gather | solution.py:69
  7.9 121.9 %all-gather.11.cloned.1.call-start = ((), (), s32[]{:S(2)}) async-start(), calls=%async_computation.5 | async-start | bytes 9437184 | tf_op jit(solution)/shard_map/all_gather | solution.py:85
  57.7 7.5 copy-start.47
  59.7 22.6 %copy-start.36 = (f32[1536]{0:T(1024)}, f32[1536]{0:T(1024)S(1)}, u32[]{:S(2)}) copy-start(f32[1536]{0:T(1024)S(1)} %div.56) | copy-start | bytes 18436
  62.3 20.1 %copy-start.44 = (f32[1536]{0:T(1024)}, f32[1536]{0:T(1024)S(1)}, u32[]{:S(2)}) copy-start(f32[1536]{0:T(1024)S(1)} %add.295) | copy-start | bytes 18436
  82.3 5.1 copy-start.14
  96.6 40.1 %all-gather.13.cloned.1.call-start = ((), (), s32[]{:S(2)}) async-start(), calls=%async_computation.6 | async-start | bytes 9437184 | tf_op jit(solution)/shard_map/all_gather | solution.py:86
  105.3 11.2 %copy-start.17 = (s32[3,512]{1,0:T(4,128)S(1)}, s32[3,512]{1,0:T(4,128)}, u32[]{:S(2)}) copy-start(s32[3,512]{1,0:T(4,128)} %param.26) | copy-start | bytes 18436
  105.3 13.0 %copy-start.6 = (bf16[3,512,768]{2,1,0:T(8,128)(2,1)S(1)}, bf16[3,512,768]{2,1,0:T(8,128)(2,1)}, u32[]{:S(2)}) copy-start(bf16[3,512,768]{2,1,0:T(8,128)(2,1)} %param.27) | copy-start | bytes 7077892
  112.3 121.5 %all-gather.15.cloned.1.call-start = ((), (), s32[]{:S(2)}) async-start(), calls=%async_computation.7 | async-start | bytes 1216512 | tf_op jit(solution)/shard_map/all_gather | solution.py:71
  112.9 140.1 %all-gather.17.cloned.1.call-start = ((), (), s32[]{:S(2)}) async-start(), calls=%async_computation.8 | async-start | bytes 4866048 | tf_op jit(solution)/shard_map/all_gather | solution.py:113
  113.5 204.6 %all-gather.19.cloned.1.call-start = ((), (), s32[]{:S(2)}) async-start(), calls=%async_computation.9 | async-start | bytes 4866048 | tf_op jit(solution)/shard_map/all_gather | solution.py:115
  114.0 405.6 %all-gather.21.cloned.1.call-start = ((), (), s32[]{:S(2)}) async-start(), calls=%async_computation.10 | async-start | bytes 9437184 | tf_op jit(solution)/shard_map/all_gather | solution.py:188
  129.8 397.0 %all-gather.23.cloned.1.call-start = ((), (), s32[]{:S(2)}) async-start(), calls=%async_computation.11 | async-start | bytes 9437184 | tf_op jit(solution)/shard_map/all_gather | solution.py:189
  225.0 8.7 copy-start
  225.0 8.7 copy-start.15
  225.0 8.7 copy-start.23
  225.1 8.6 copy-start.25
  231.5 2.2 copy-start.55
  238.9 14.0 %copy-start.51 = (f32[768]{0:T(1024)S(1)}, f32[768]{0:T(1024)}, u32[]{:S(2)}) copy-start(f32[768]{0:T(1024)} %convert_element_type.156) | copy-start | bytes 9220
  239.0 14.0 %copy-start.52 = (f32[3072]{0:T(1024)S(1)}, f32[3072]{0:T(1024)}, u32[]{:S(2)}) copy-start(f32[3072]{0:T(1024)} %convert_element_type.159) | copy-start | bytes 36868
  239.0 14.0 %copy-start.54 = (f32[768]{0:T(1024)S(1)}, f32[768]{0:T(1024)}, u32[]{:S(2)}) copy-start(f32[768]{0:T(1024)} %convert_element_type.157) | copy-start | bytes 9220
  242.4 75.7 %copy-start.21 = (bf16[1536,768]{1,0:T(8,128)(2,1)S(1)}, bf16[1536,768]{1,0:T(8,128)(2,1)}, u32[]{:S(2)}) copy-start(bf16[1536,768]{1,0:T(8,128)(2,1)} %bitcast_convert_fusion.4) | copy-start | bytes 7077892
  318.1 23.9 %copy-start.12 = (f32[1536,768]{1,0:T(8,128)S(1)}, f32[1536,768]{1,0:T(8,128)}, u32[]{:S(2)}) copy-start(f32[1536,768]{1,0:T(8,128)} %copy-done.11) | copy-start | bytes 14155780
  342.0 13.4 %copy-start.43 = (f32[1536]{0:T(1024)S(1)}, f32[1536]{0:T(1024)}, u32[]{:S(2)}) copy-start(f32[1536]{0:T(1024)} %copy-done.42) | copy-start | bytes 18436
  355.5 2.3 copy-start.7
  357.7 2.3 copy-start.5
  357.8 2.2 copy-start.40
  357.8 3.6 copy-start.59
  365.6 8.5 copy-start.26
  384.6 6.2 copy-start.10
  384.6 388.3 %reduce-scatter.7.cloned.1.call-start = ((), (), s32[]{:S(2)}) async-start(), calls=%async_computation.13 | async-start | bytes 2433024 | tf_op jit(solution)/shard_map/reduce_scatter | solution.py:232
  390.7 382.2 %reduce-scatter.9.cloned.1.call-start = ((), (), s32[]{:S(2)}) async-start(), calls=%async_computation.14 | async-start | bytes 9732096 | tf_op jit(solution)/shard_map/reduce_scatter | solution.py:146
  390.8 7.7 copy-start.9
  390.8 10.6 %slice-start = ((s8[4718592]{0:T(1024)(128)(4,1)}), s8[4194304]{0:T(1024)(128)(4,1)S(1)}, s32[]{:S(2)}) async-start(s8[4718592]{0:T(1024)(128)(4,1)} %bitcast.186), calls=%async_computation.16 | async-start | bytes 8388608
  392.9 7.8 copy-start.16
  392.9 8.5 slice-start.1
  414.5 376.6 %reduce-scatter.11.cloned.1.call-start = ((), (), s32[]{:S(2)}) async-start(), calls=%async_computation.15 | async-start | bytes 9732096 | tf_op jit(solution)/shard_map/reduce_scatter | solution.py:148
  502.6 2.9 copy-start.32
  502.6 6.7 copy-start.60
  504.6 4.7 copy-start.22
  519.6 396.9 %reduce-scatter.5.cloned.1.call-start = ((), (), s32[]{:S(2)}) async-start(), calls=%async_computation.12 | async-start | bytes 7299072 | tf_op jit(solution)/shard_map/reduce_scatter | solution.py:230
  526.8 7.3 copy-start.2
  668.6 3.7 slice-start.2
  669.4 2.9 slice-start.3
  672.3 3.5 copy-start.20
  672.6 3.1 copy-start.27
  683.7 2.9 copy-start.28
  683.7 2.9 copy-start.33
  683.7 3.6 copy-start.30
  683.7 5.3 copy-start.29
  683.7 5.3 copy-start.34
  683.7 6.0 copy-start.49
  689.8 14.1 %copy-start.4 = (bf16[3,512,768]{2,1,0:T(8,128)(2,1)S(1)}, bf16[3,512,768]{2,1,0:T(8,128)(2,1)}, u32[]{:S(2)}) copy-start(bf16[3,512,768]{2,1,0:T(8,128)(2,1)} %param.25) | copy-start | bytes 7077892
  689.8 14.1 %copy-start.37 = (f32[1536]{0:T(1024)S(1)}, f32[1536]{0:T(1024)}, u32[]{:S(2)}) copy-start(f32[1536]{0:T(1024)} %copy-done.36) | copy-start | bytes 18436
  689.8 14.1 %copy-start.48 = (f32[768]{0:T(1024)S(1)}, f32[768]{0:T(1024)}, u32[]{:S(2)}) copy-start(f32[768]{0:T(1024)} %copy-done.47) | copy-start | bytes 9220
  704.0 10.0 %copy-start.45 = (f32[1536]{0:T(1024)S(1)}, f32[1536]{0:T(1024)}, u32[]{:S(2)}) copy-start(f32[1536]{0:T(1024)} %copy-done.44) | copy-start | bytes 18436
  704.0 12.1 %copy-start.39 = (f32[1536]{0:T(1024)S(1)}, f32[1536]{0:T(1024)}, u32[]{:S(2)}) copy-start(f32[1536]{0:T(1024)} %copy-done.38) | copy-start | bytes 18436
  713.9 4.7 copy-start.50
  713.9 4.7 copy-start.53
  713.9 4.7 copy-start.56
  713.9 4.7 copy-start.57
  714.0 50.7 %copy-start.41 = (f32[1536]{0:T(1024)S(1)}, f32[1536]{0:T(1024)}, u32[]{:S(2)}) copy-start(f32[1536]{0:T(1024)} %copy-done.40) | copy-start | bytes 18436
  (13 other events, 19.6 us)
Sparse Core Ops, SparseCore 0:
  10.9 62.8 all-gather.8
  96.7 14.4 all-gather.10
  112.8 16.8 all-gather.12
  132.4 55.2 all-gather.14
  190.4 62.4 all-gather.16
  255.7 62.3 all-gather.18
  319.6 14.4 all-gather.20
  384.7 16.3 all-gather.22
  407.0 100.3 reduce-scatter.6
  514.7 134.6 reduce-scatter.8
  655.8 135.2 reduce-scatter.10
  798.1 118.2 reduce-scatter.4
where the time goes:
time: 932 us; the launch traced here: 924 us
  matrix products  454 us (49%)
  waiting for transfers between devices  176 us (19%)
  local copies, waits for them, and re-layouts  119 us (13%)
  blocking collectives  88.3 us (9%)
  other arithmetic  68.1 us (7%)
  between operations  15.3 us (2%)
    reduce_scatter x1, waiting for transfers between devices, on_device(): lax.psum_scatter(grad_wqkv, ('seq', 'rows'), scatter_dimension=0, tiled=T...  125 us
    dot_general x6, matrix products, scores(): jnp.einsum('rqhe,rkhe->rqhk', query_part, key_part, preferred_element_typ...  107 us
    unnamed x2, blocking collectives  84.3 us
    unnamed x169, local copies, waits for them, and re-layouts  78.2 us
    dot_general x1, matrix products, on_device(): jnp.dot(normed_two_low, w_up, preferred_element_type=f32) + b_up.astype(f32)  54.3 us
    dot_general x2, matrix products, key_advance(): jnp.einsum('rqhk,rqhe->rkhe', grad_score, query_block, preferred_element_...  47.8 us
    dot_general x2, matrix products, query_advance(): jnp.einsum('rqhk,rkhe->rqhe', grad_score, key_block, preferred_element_ty...  47.1 us
    dot_general x2, matrix products, key_advance(): jnp.einsum('rqhk,rqhe->rkhe', expo.astype(bf16), grad_block, preferred_el...  41.3 us
  transfers between devices with their start and end apart: 12, of which 5 were waited for; matrix products, arithmetic and copies ran while one was open for 65% of the time, Pallas kernels for 0%

commit v1 on v0

--- a/solution.py
+++ b/solution.py
@@ -1,6 +1,11 @@
+import functools
+
 import jax
 import jax.numpy as jnp
 from jax import lax
+from jax.experimental import pallas as pl
+from jax.experimental.pallas import tpu as pltpu
+from jax.sharding import Mesh
 from jax.sharding import PartitionSpec as P
 
 HEADS = 12
@@ -258,51 +263,771 @@
     )
 
 
+f32 = jnp.float32
+bf16 = jnp.bfloat16
+NT = (((1,), (1,)), ((), ()))
+LOG2E = 1.4426950408889634
+SCORE = 0.125 * LOG2E
+BIG = 16384.0
+VMEM_BYTES = 60 * 1024 * 1024
+TQ_F, TK_F = 256, 256
+TK_B, TQ_B = 128, 256
+LANE_LOG = 41
+LANE_PAD = 44
+
+
+def kernel_params(flops, bytes_accessed, transcendentals=0, order=("arbitrary",)):
+    return dict(
+        compiler_params=pltpu.CompilerParams(
+            vmem_limit_bytes=VMEM_BYTES, dimension_semantics=order
+        ),
+        cost_estimate=pl.CostEstimate(
+            flops=int(flops), bytes_accessed=int(bytes_accessed), transcendentals=int(transcendentals)
+        ),
+    )
+
+
+def standardise(value):
+    middle = jnp.mean(value, axis=-1, keepdims=True)
+    centred = value - middle
+    spread = jnp.mean(centred * centred, axis=-1, keepdims=True)
+    rstd = lax.rsqrt(spread + 1e-06)
+    return centred * rstd, rstd
+
+
+def norm_pull(grad_normed, gain, xhat, rstd):
+    scaled = grad_normed * gain
+    first = jnp.mean(scaled, axis=-1, keepdims=True)
+    second = jnp.mean(scaled * xhat, axis=-1, keepdims=True)
+    return rstd * (scaled - first - xhat * second)
+
+
+def gelu_pair(x):
+    size = jnp.abs(x)
+    t = 1.0 / (1.0 + 0.23164189 * size)
+    bell = jnp.exp2(x * x * (-0.5 * LOG2E))
+    poly = t * (0.127414796 + t * (-0.142248368 + t * (0.7107068705 + t * (-0.7265760135 + t * 0.5307027145))))
+    tail = poly * bell
+    phi = jnp.where(x >= 0.0, 1.0 - tail, tail)
+    return x * phi, phi + x * bell * 0.3989422804014327
+
+
+def project_kernel(own_ref, other_ref, w_ref, pack_ref, shift_ref, normed_ref, mixed_ref):
+    which = pl.program_id(0)
+    value = jnp.where(which == 0, own_ref[0].astype(f32), other_ref[0].astype(f32))
+    xhat, _ = standardise(value)
+    normed = (xhat * pack_ref[0:1, :] + pack_ref[1:2, :]).astype(bf16)
+    normed_ref[0, 0] = normed
+    mixed = jnp.dot(normed, w_ref[...], preferred_element_type=f32) + shift_ref[...]
+    mixed_ref[0, 0] = mixed.astype(bf16)
+
+
+def attend_kernel(flag_ref, mixed_ref, qx_ref, kx_ref, out_ref, lse_ref, q_s, k_s, v_s, acc_s):
+    row = pl.program_id(0)
+    length = q_s.shape[1]
+    heads = q_s.shape[0]
+    wide = heads * HEAD_DIM
+    half = length // 2
+    low = lax.broadcasted_iota(jnp.int32, (length, 128), 1) < HEAD_DIM
+    qx = qx_ref[0].astype(f32)
+    kx = kx_ref[0].astype(f32)
+    for pair in range(heads // 2):
+        lanes = slice(128 * pair, 128 * pair + 128)
+        q = mixed_ref[:, 0, :, lanes].reshape(length, 128).astype(f32)
+        k = mixed_ref[:, 0, :, wide + 128 * pair : wide + 128 * pair + 128].reshape(length, 128).astype(f32)
+        v = mixed_ref[:, 0, :, 2 * wide + 128 * pair : 2 * wide + 128 * pair + 128].reshape(length, 128).astype(f32)
+        q_s[2 * pair] = jnp.where(low, q, qx).astype(bf16)
+        q_s[2 * pair + 1] = jnp.where(low, qx, q).astype(bf16)
+        k_s[2 * pair] = jnp.where(low, k, kx).astype(bf16)
+        k_s[2 * pair + 1] = jnp.where(low, kx, k).astype(bf16)
+        v_s[2 * pair] = jnp.where(low, v, 1.0).astype(bf16)
+        v_s[2 * pair + 1] = jnp.where(low, 1.0, v).astype(bf16)
+    acc_s[...] = jnp.zeros_like(acc_s)
+    key_blocks = length // TK_F
+
+    def step(index, carry):
+        @pl.when(flag_ref[row, index] != 0)
+        def _():
+            q_at = pl.ds(pl.multiple_of((index // key_blocks) * TQ_F, TQ_F), TQ_F)
+            k_at = pl.ds(pl.multiple_of((index % key_blocks) * TK_F, TK_F), TK_F)
+            for head in range(heads):
+                score = lax.dot_general(
+                    q_s[head, q_at, :], k_s[head, k_at, :], NT, preferred_element_type=f32
+                )
+                expo = jnp.exp2(score * SCORE).astype(bf16)
+                acc_s[head, q_at, :] += jnp.dot(expo, v_s[head, k_at, :], preferred_element_type=f32)
+
+        return carry
+
+    lax.fori_loop(0, (length // TQ_F) * key_blocks, step, 0)
+    for pair in range(heads // 2):
+        lanes = slice(128 * pair, 128 * pair + 128)
+        first, second = acc_s[2 * pair], acc_s[2 * pair + 1]
+        top = jnp.where(low, first, second)
+        crossed = jnp.where(low, second, first)
+        totals = pltpu.roll(crossed, HEAD_DIM, 1)
+        attended = (top / totals).astype(bf16)
+        lse = 8.0 * jnp.log(crossed)
+        for side in range(2):
+            out_ref[side, 0, :, lanes] = attended[side * half : (side + 1) * half]
+            lse_ref[side, 0, :, lanes] = lse[side * half : (side + 1) * half]
+
+
+def forward_kernel(
+    side_ref, x_ref, mine_ref, recv_ref, wo_ref, up_ref, down_ref, grad_ref, pack_ref,
+    out_ref, middle_ref, normed_ref, slope_ref, gdown_ref, bias_ref, acc_s,
+):
+    turn = pl.program_id(0)
+    side = side_ref[0]
+    chunks = acc_s.shape[0]
+    size = acc_s.shape[2]
+    middle = (
+        x_ref[0].astype(f32)
+        + jnp.dot(mine_ref[0, 0], wo_ref[side], preferred_element_type=f32)
+        + jnp.dot(recv_ref[0], wo_ref[1 - side], preferred_element_type=f32)
+        + pack_ref[2:3, :]
+    )
+    middle_ref[0] = middle
+    xhat, _ = standardise(middle)
+    normed = (xhat * pack_ref[3:4, :] + pack_ref[4:5, :]).astype(bf16)
+    normed_ref[0] = normed
+    grad = grad_ref[0]
+    grad_t = grad.T
+    total = middle + pack_ref[5:6, :]
+
+    @pl.when(turn == 0)
+    def _():
+        acc_s[...] = jnp.zeros_like(acc_s)
+        bias_ref[...] = jnp.zeros_like(bias_ref)
+
+    bias_ref[0:1, :] += jnp.sum(grad.astype(f32), axis=0, keepdims=True)
+    for f in range(chunks):
+        at = slice(f * size, (f + 1) * size)
+        pre = jnp.dot(normed, up_ref[:, at], preferred_element_type=f32) + pack_ref[8 + f : 9 + f, :]
+        hidden, slope = gelu_pair(pre)
+        slope_ref[0, :, at] = slope.astype(bf16)
+        hidden = hidden.astype(bf16)
+        total = total + jnp.dot(hidden, down_ref[at, :], preferred_element_type=f32)
+        acc_s[f] += jnp.dot(grad_t, hidden, preferred_element_type=f32)
+    out_ref[0] = total.astype(bf16)
+
+    @pl.when(turn == pl.num_programs(0) - 1)
+    def _():
+        half = chunks // 2
+        for f in range(chunks):
+            target = jnp.where(side == f // half, 0, 1)
+            gdown_ref[target, f % half] = acc_s[f].T.astype(bf16)
+
+
+def backward_kernel(
+    side_ref, grad_ref, slope_ref, up_ref, down_ref, normed_ref, middle_ref, pack_ref,
+    gmid_ref, glow_ref, gup_ref, gbias_ref, gnorm_ref, acc_s,
+):
+    turn = pl.program_id(0)
+    side = side_ref[0]
+    chunks = acc_s.shape[0]
+    size = acc_s.shape[2]
+    grad = grad_ref[0]
+    normed_t = normed_ref[0].T
+
+    @pl.when(turn == 0)
+    def _():
+        acc_s[...] = jnp.zeros_like(acc_s)
+        gbias_ref[...] = jnp.zeros_like(gbias_ref)
+        gnorm_ref[...] = jnp.zeros_like(gnorm_ref)
+
+    gnormed = None
+    for f in range(chunks):
+        at = slice(f * size, (f + 1) * size)
+        ghidden = lax.dot_general(grad, down_ref[at, :], NT, preferred_element_type=f32)
+        gpre = (ghidden * slope_ref[0, :, at].astype(f32)).astype(bf16)
+        gbias_ref[f] += jnp.sum(gpre.astype(f32), axis=0, keepdims=True)
+        part = lax.dot_general(gpre, up_ref[:, at], NT, preferred_element_type=f32)
+        gnormed = part if gnormed is None else gnormed + part
+        acc_s[f] += jnp.dot(normed_t, gpre, preferred_element_type=f32)
+    xhat, rstd = standardise(middle_ref[0])
+    gmid = grad.astype(f32) + norm_pull(gnormed, pack_ref[3:4, :], xhat, rstd)
+    gmid_ref[0] = gmid
+    low = gmid.astype(bf16)
+    glow_ref[0] = low
+    gnorm_ref[0:1, :] += jnp.sum(gnormed * xhat, axis=0, keepdims=True)
+    gnorm_ref[1:2, :] += jnp.sum(gnormed, axis=0, keepdims=True)
+    gnorm_ref[2:3, :] += jnp.sum(low.astype(f32), axis=0, keepdims=True)
+
+    @pl.when(turn == pl.num_programs(0) - 1)
+    def _():
+        rows = acc_s.shape[1] // 2
+        mine = pl.ds(pl.multiple_of(side * rows, rows), rows)
+        other = pl.ds(pl.multiple_of((1 - side) * rows, rows), rows)
+        for f in range(chunks):
+            gup_ref[0, f] = acc_s[f, mine, :].astype(bf16)
+            gup_ref[1, f] = acc_s[f, other, :].astype(bf16)
+
+
+def attend_back_kernel(
+    flag_ref, mixed_ref, lse_ref, att_ref, own_ref, other_ref, wo_ref, qx_ref, kx_ref,
+    gmixed_ref, gout_ref, gbias_ref,
+    q_s, k_s, v_s, d_s, qz_s, dz_s, kt_s, gq_s, gk_s, gv_s, go_s,
+):
+    row = pl.program_id(0)
+    heads, length = q_s.shape[0], q_s.shape[1]
+    wide = heads * HEAD_DIM
+    half = length // 2
+    lane = lax.broadcasted_iota(jnp.int32, (length, 128), 1)
+    low = lane < HEAD_DIM
+    place = lane % HEAD_DIM
+    square_row = lax.broadcasted_iota(jnp.int32, (128, 128), 0) < HEAD_DIM
+    square_col = lax.broadcasted_iota(jnp.int32, (128, 128), 1) < HEAD_DIM
+    crossing = jnp.where(square_row == square_col, 0.0, 1.0).astype(bf16)
+    qx = qx_ref[0].astype(f32)
+    kx = kx_ref[0].astype(f32)
+    vx = jnp.where(place < 2, 1.0, 0.0)
+
+    @pl.when(row == 0)
+    def _():
+        go_s[...] = jnp.zeros_like(go_s)
+        gbias_ref[...] = jnp.zeros_like(gbias_ref)
+
+    att = att_ref[:, 0].reshape(length, wide)
+    gates = jnp.concatenate([own_ref[0], other_ref[0]], axis=0)
+    go_s[...] += jnp.dot(att.T, gates, preferred_element_type=f32)
+    gatt = lax.dot_general(gates, wo_ref[...], NT, preferred_element_type=f32)
+    for pair in range(heads // 2):
+        lanes = slice(128 * pair, 128 * pair + 128)
+        q = mixed_ref[:, 0, :, lanes].reshape(length, 128).astype(f32)
+        k = mixed_ref[:, 0, :, wide + 128 * pair : wide + 128 * pair + 128].reshape(length, 128).astype(f32)
+        v = mixed_ref[:, 0, :, 2 * wide + 128 * pair : 2 * wide + 128 * pair + 128].reshape(length, 128).astype(f32)
+        lse = -lse_ref[:, 0, :, lanes].reshape(length, 128)
+        lse_a = lse.astype(bf16).astype(f32)
+        lse_b = (lse - lse_a).astype(bf16).astype(f32)
+        lse_c = lse - lse_a - lse_b
+        ext = jnp.where(
+            place == LANE_LOG,
+            lse_a,
+            jnp.where(place == LANE_LOG + 1, lse_b, jnp.where(place == LANE_LOG + 2, lse_c, qx)),
+        )
+        q_s[2 * pair] = jnp.where(low, q, ext).astype(bf16)
+        q_s[2 * pair + 1] = jnp.where(low, ext, q).astype(bf16)
+        k_s[2 * pair] = jnp.where(low, k, kx).astype(bf16)
+        k_s[2 * pair + 1] = jnp.where(low, kx, k).astype(bf16)
+        v_s[2 * pair] = jnp.where(low, v, vx).astype(bf16)
+        v_s[2 * pair + 1] = jnp.where(low, vx, v).astype(bf16)
+        d = gatt[:, lanes]
+        moved = d * att[:, lanes].astype(f32)
+        moved_a = moved.astype(bf16)
+        moved_b = (moved - moved_a.astype(f32)).astype(bf16)
+        shift = -(
+            jnp.dot(moved_a, crossing, preferred_element_type=f32)
+            + jnp.dot(moved_b, crossing, preferred_element_type=f32)
+        )
+        shift_a = shift.astype(bf16).astype(f32)
+        dx = jnp.where(place == 0, shift_a, jnp.where(place == 1, shift - shift_a, 0.0))
+        d_s[2 * pair] = jnp.where(low, d, dx).astype(bf16)
+        d_s[2 * pair + 1] = jnp.where(low, dx, d).astype(bf16)
+        qa, qb = jnp.where(low, q, 0.0).astype(bf16), jnp.where(low, 0.0, q).astype(bf16)
+        da, db = jnp.where(low, d, 0.0).astype(bf16), jnp.where(low, 0.0, d).astype(bf16)
+        for i in range(length // TQ_B):
+            at = slice(i * TQ_B, (i + 1) * TQ_B)
+            qz_s[pair, i, :TQ_B] = qa[at]
+            qz_s[pair, i, TQ_B:] = qb[at]
+            dz_s[pair, i, :TQ_B] = da[at]
+            dz_s[pair, i, TQ_B:] = db[at]
+        kt = k.T.astype(bf16)
+        for i in range(length // TK_B):
+            kt_s[i, lanes, :] = kt[:, i * TK_B : (i + 1) * TK_B]
+    gq_s[...] = jnp.zeros_like(gq_s)
+    gk_s[...] = jnp.zeros_like(gk_s)
+    gv_s[...] = jnp.zeros_like(gv_s)
+    query_blocks = length // TQ_B
+
+    def step(index, carry):
+        @pl.when(flag_ref[row, index] != 0)
+        def _():
+            qi = index % query_blocks
+            ki = index // query_blocks
+            q_at = pl.ds(pl.multiple_of(qi * TQ_B, TQ_B), TQ_B)
+            k_at = pl.ds(pl.multiple_of(ki * TK_B, TK_B), TK_B)
+            for pair in range(heads // 2):
+                probs, grads = [], []
+                for head in (2 * pair, 2 * pair + 1):
+                    score = lax.dot_general(
+                        k_s[head, k_at, :], q_s[head, q_at, :], NT, preferred_element_type=f32
+                    )
+                    prob = jnp.exp2(score * SCORE)
+                    inner = lax.dot_general(
+                        v_s[head, k_at, :], d_s[head, q_at, :], NT, preferred_element_type=f32
+                    )
+                    gscore = (prob * inner).astype(bf16)
+                    probs.append(prob.astype(bf16))
+                    grads.append(gscore)
+                    at = slice(head * HEAD_DIM, (head + 1) * HEAD_DIM)
+                    gq_s[qi, at, :] += jnp.dot(kt_s[ki, at, :], gscore, preferred_element_type=f32)
+                gv_s[pair, k_at, :] += jnp.dot(
+                    jnp.concatenate(probs, axis=1), dz_s[pair, qi], preferred_element_type=f32
+                )
+                gk_s[pair, k_at, :] += jnp.dot(
+                    jnp.concatenate(grads, axis=1), qz_s[pair, qi], preferred_element_type=f32
+                )
+
+        return carry
+
+    lax.fori_loop(0, query_blocks * (length // TK_B), step, 0)
+    for i in range(query_blocks):
+        gq = (0.125 * gq_s[i].T).astype(bf16)
+        at = (i * TQ_B) % half
+        gmixed_ref[(i * TQ_B) // half, 0, at : at + TQ_B, 0:wide] = gq
+        gbias_ref[0:1, 0:wide] += jnp.sum(gq.astype(f32), axis=0, keepdims=True)
+    for pair in range(heads // 2):
+        gk = (0.125 * gk_s[pair]).astype(bf16)
+        gv = gv_s[pair].astype(bf16)
+        k_lanes = slice(wide + 128 * pair, wide + 128 * pair + 128)
+        v_lanes = slice(2 * wide + 128 * pair, 2 * wide + 128 * pair + 128)
+        gbias_ref[0:1, v_lanes] += jnp.sum(gv.astype(f32), axis=0, keepdims=True)
+        for side in range(2):
+            gmixed_ref[side, 0, :, k_lanes] = gk[side * half : (side + 1) * half]
+            gmixed_ref[side, 0, :, v_lanes] = gv[side * half : (side + 1) * half]
+
+    @pl.when(row == pl.num_programs(0) - 1)
+    def _():
+        gout_ref[...] = go_s[...].astype(bf16)
+
+
+def input_kernel(gmixed_ref, w_ref, recv_ref, x_ref, gmid_ref, pack_ref, ginput_ref, gnorm_ref):
+    turn = pl.program_id(0)
+    gnormed = lax.dot_general(gmixed_ref[0, 0], w_ref[...], NT, preferred_element_type=f32)
+    gnormed = gnormed + recv_ref[0].astype(f32)
+    xhat, rstd = standardise(x_ref[0].astype(f32))
+    ginput_ref[0] = gmid_ref[0] + norm_pull(gnormed, pack_ref[0:1, :], xhat, rstd)
+
+    @pl.when(turn == 0)
+    def _():
+        gnorm_ref[...] = jnp.zeros_like(gnorm_ref)
+
+    gnorm_ref[0:1, :] += jnp.sum(gnormed * xhat, axis=0, keepdims=True)
+    gnorm_ref[1:2, :] += jnp.sum(gnormed, axis=0, keepdims=True)
+
+
+def partner(value):
+    return lax.ppermute(value, "seq", [(0, 1), (1, 0)])
+
+
+def exchange(value, axis):
+    return lax.all_to_all(value, axis, 0, 0, tiled=True)
+
+
+def spread_line(value, lines):
+    return exchange(jnp.broadcast_to(value[None], (lines,) + value.shape), "line")
+
+
+def flip(value, axis):
+    return lax.ppermute(value, axis, [(0, 1), (1, 0)])
+
+
+def in_order(index, own, received):
+    return jnp.where(index == 0, jnp.stack([own, received]), jnp.stack([received, own]))
+
+
+def spread_plane(value, axes):
+    first, second = axes
+    pairs = in_order(lax.axis_index(first), value, flip(value, first))
+    return pairs, flip(pairs, second)
+
+
+def after(value, *others):
+    return lax.optimization_barrier((value,) + others)[0]
+
+
+def place(pieces, spots, axes, rows, cols):
+    moved = [jnp.swapaxes(piece[:, :, rows, cols], 0, 1) for piece in pieces]
+    out = None
+    for piece, (side, spot) in zip(moved, spots):
+        if axes == ("x", "y"):
+            piece, start = piece[None, :, None], (side, 0, spot, 0, 0, 0)
+            whole = (2, piece.shape[1], 2, 2) + piece.shape[4:]
+        else:
+            piece, start = piece[None, :, :, None], (side, 0, 0, spot, 0, 0)
+            whole = (2, piece.shape[1], 2, 2) + piece.shape[4:]
+        if out is None:
+            out = jnp.broadcast_to(piece, whole)
+        else:
+            out = lax.dynamic_update_slice(out, piece, start)
+    return out
+
+
+def sum_rows(value):
+    across = jnp.sum(exchange(value, ("y", "x")).astype(f32), axis=0).astype(bf16)
+    return jnp.sum(exchange(across, "line").astype(f32), axis=0)
+
+
+def masks(seg, pos):
+    pad = seg == CLIPS - 1
+    lane = jnp.arange(128, dtype=jnp.int32) % HEAD_DIM
+    seg, pos, pad = seg[..., None], pos[..., None], pad[..., None]
+    clip_lane = lane < CLIPS - 1
+    digit = jnp.where(lane < 9, pos // 256, jnp.where(lane < 25, (pos // 16) % 16, pos % 16))
+    digit_base = jnp.where(lane < 9, 5, jnp.where(lane < 25, 9, 25))
+    digit_lane = (lane >= 5) & (lane < LANE_LOG)
+    hit_clip = lane == seg
+    hit_digit = lane - digit_base == digit
+    log_lane = (lane >= LANE_LOG) & (lane < LANE_PAD)
+    pad_lane = lane == LANE_PAD
+    bad = (clip_lane & ~hit_clip) | (digit_lane & pad & ~hit_digit) | (pad_lane & ~pad)
+    qx = jnp.where(bad, -BIG, 0.0).astype(bf16)
+    on = (clip_lane & hit_clip) | (digit_lane & pad & hit_digit) | log_lane | (pad_lane & pad)
+    kx = jnp.where(on, 1.0, 0.0).astype(bf16)
+    return qx, kx
+
+
+def block_flags(ident, rows_block, cols_block):
+    count, length = ident.shape
+    by_row = ident.reshape(count, length // rows_block, rows_block)
+    by_col = ident.reshape(count, length // cols_block, cols_block)
+    low_row, high_row = jnp.min(by_row, axis=2)[:, :, None], jnp.max(by_row, axis=2)[:, :, None]
+    low_col, high_col = jnp.min(by_col, axis=2)[:, None, :], jnp.max(by_col, axis=2)[:, None, :]
+    meets = (low_row <= high_col) & (low_col <= high_row)
+    return meets.astype(jnp.int32).reshape(count, -1)
+
+
+def pair_device(
+    lines, planes,
+    tokens, segment_ids, cotangent, ln1_gain, ln1_bias, qkv_weight, qv_bias, out_weight, out_bias,
+    ln2_gain, ln2_bias, up_weight, up_bias, down_weight, down_bias, avg_qkv, avg_out, avg_up, avg_down,
+):
+    count, part, width = tokens.shape
+    length = 2 * part
+    wide = width // 2
+    heads = HEADS // 2
+    hidden_width = up_weight.shape[1]
+    chunks = hidden_width // width
+    share = qkv_weight.shape[0]
+    side = lax.axis_index("seq").astype(jnp.int32)
+    first = side == 0
+    side_arr = side.reshape(1)
+    const = lambda *shape: pl.BlockSpec(shape, lambda *_: (0,) * len(shape), pipeline_mode=pl.Buffered(1))
+    row_block = lambda *shape: pl.BlockSpec((1,) + shape, lambda j, *_: (j,) + (0,) * len(shape))
+    both_block = lambda lanes: pl.BlockSpec((2, 1, part, lanes), lambda j, *_: (0, j, 0, 0))
+    own_block = lambda lanes: pl.BlockSpec((1, 1, part, lanes), lambda j, *_: (0, j, 0, 0))
+
+    split_cols = qkv_weight.reshape(share, 3, 2, wide)
+    pick = lambda which: lax.dynamic_index_in_dim(split_cols, which, 2, keepdims=False).reshape(share, 3 * wide)
+    small = jnp.stack([ln1_gain, ln1_bias, out_bias, ln2_gain, ln2_bias, down_bias], axis=0)
+    small = jnp.concatenate([small, qv_bias.reshape(2, share), up_bias.reshape(chunks, share)], axis=0)
+    small_rows = small.shape[0]
+    small = jnp.pad(small.T, ((0, 0), (0, 128 - small_rows)))
+    mine = jnp.concatenate([pick(side), small], axis=1)
+    give = jnp.concatenate([pick(1 - side), small], axis=1)
+    take = partner(give)
+    tokens_other = partner(tokens)
+    seg_other = partner(segment_ids)
+    start = jnp.where(first, jnp.stack([mine, take]), jnp.stack([take, mine]))
+    x_at, y_at = lax.axis_index("x"), lax.axis_index("y")
+    first_line = spread_line(start, lines)
+    one_m, one_r = spread_plane(first_line[:, 0], ("x", "y"))
+    two_m, two_r = spread_plane(first_line[:, 1], ("y", "x"))
+    one = in_order(y_at, one_m, one_r).transpose(2, 0, 1, 3, 4)
+    two = in_order(x_at, two_m, two_r).transpose(2, 1, 0, 3, 4)
+    first_all = jnp.stack([one, two])
+    w_qkv = first_all[..., : 3 * wide].reshape(width, 3 * wide)
+    small_all = jnp.moveaxis(first_all[..., 3 * wide : 3 * wide + small_rows].astype(f32), -1, -2)
+    vector = lambda i: small_all[..., i, :].reshape(width)
+    bias_qv = small_all[..., 6:8, :].reshape(2 * width)
+    bias_up = small_all[..., 8 : 8 + chunks, :].reshape(chunks, width)
+    pack = jnp.concatenate(
+        [jnp.stack([vector(i) for i in range(6)]), jnp.zeros((2, width), f32), bias_up, jnp.zeros((4, width), f32)],
+        axis=0,
+    )
+    bias_here = lambda base: lax.dynamic_slice_in_dim(bias_qv, base + side * wide, wide, 0)
+    shift = jnp.concatenate([bias_here(0), jnp.zeros((wide,), f32), bias_here(width)])[None]
+
+    up_start, down_start = up_weight, jnp.concatenate([down_weight, out_weight], axis=0)
+    up_line = spread_line(after(up_start, first_line), lines)
+    down_line = spread_line(after(down_start, up_line), lines)
+    up_line, down_line = after(up_line, one_r, two_r), after(down_line, one_r, two_r)
+    up_pieces = spread_plane(up_line, ("x", "y"))
+    down_pieces = spread_plane(down_line, ("y", "x"))
+    up_pieces += (partner(up_pieces[0]), partner(up_pieces[1]))
+    down_pieces += (partner(down_pieces[0]), partner(down_pieces[1]))
+    up_spots = ((side, y_at), (side, 1 - y_at), (1 - side, y_at), (1 - side, 1 - y_at))
+    down_spots = ((side, x_at), (side, 1 - x_at), (1 - side, x_at), (1 - side, 1 - x_at))
+    own_rows, every = chunks * share, slice(None)
+    w_up = place(up_pieces, up_spots, ("x", "y"), every, every).reshape(width, hidden_width)
+    w_down = place(down_pieces, down_spots, ("y", "x"), slice(0, own_rows), every).reshape(hidden_width, width)
+    w_out = place(down_pieces, down_spots, ("y", "x"), slice(own_rows, None), every).reshape(2, wide, width)
+    wo_mine = lax.dynamic_index_in_dim(w_out, side, 0, keepdims=False)
+
+    seg = jnp.concatenate([segment_ids, seg_other], axis=1)
+    spots = jnp.arange(part, dtype=jnp.int32)
+    pos = jnp.concatenate([side * part + spots, (1 - side) * part + spots])
+    qx, kx = masks(seg, jnp.broadcast_to(pos, seg.shape))
+    ident = jnp.where(seg == CLIPS - 1, CLIPS + pos, seg)
+    flags_f = block_flags(ident, TQ_F, TK_F)
+    flags_b = block_flags(ident, TK_B, TQ_B)
+
+    sds = jax.ShapeDtypeStruct
+    normed, mixed = pl.pallas_call(
+        project_kernel,
+        grid=(2, count),
+        in_specs=[
+            pl.BlockSpec((1, part, width), lambda h, j: (jnp.where(h == 0, j, count - 1), 0, 0)),
+            pl.BlockSpec((1, part, width), lambda h, j: (jnp.where(h == 0, 0, j), 0, 0)),
+            const(width, 3 * wide),
+            const(16, width),
+            const(1, 3 * wide),
+        ],
+        out_specs=[
+            pl.BlockSpec((1, 1, part, width), lambda h, j: (h, j, 0, 0)),
+            pl.BlockSpec((1, 1, part, 3 * wide), lambda h, j: (h, j, 0, 0)),
+        ],
+        out_shape=[sds((2, count, part, width), bf16), sds((2, count, part, 3 * wide), bf16)],
+        name="project",
+        **kernel_params(
+            2 * 2 * count * part * width * 3 * wide, 20e6, order=("arbitrary", "arbitrary")
+        ),
+    )(tokens, tokens_other, w_qkv, pack, shift)
+
+    attended, lse = pl.pallas_call(
+        attend_kernel,
+        grid_spec=pltpu.PrefetchScalarGridSpec(
+            num_scalar_prefetch=1,
+            grid=(count,),
+            in_specs=[both_block(3 * wide), row_block(length, 128), row_block(length, 128)],
+            out_specs=[both_block(wide), both_block(wide)],
+            scratch_shapes=[pltpu.VMEM((heads, length, 128), bf16)] * 3
+            + [pltpu.VMEM((heads, length, 128), f32)],
+        ),
+        out_shape=[sds((2, count, part, wide), bf16), sds((2, count, part, wide), f32)],
+        name="attend",
+        **kernel_params(16e9, 20e6, 12e6),
+    )(flags_f, mixed, qx, kx)
+
+    attended_recv = partner(attended[1])
+
+    out_tokens, middle, normed_two, slope, gdown, gdown_bias = pl.pallas_call(
+        forward_kernel,
+        grid_spec=pltpu.PrefetchScalarGridSpec(
+            num_scalar_prefetch=1,
+            grid=(count,),
+            in_specs=[
+                row_block(part, width),
+                own_block(wide),
+                row_block(part, wide),
+                const(2, wide, width),
+                const(width, hidden_width),
+                const(hidden_width, width),
+                row_block(part, width),
+                const(16, width),
+            ],
+            out_specs=[
+                row_block(part, width),
+                row_block(part, width),
+                row_block(part, width),
+                row_block(part, hidden_width),
+                const(2, chunks // 2, width, width),
+                const(8, width),
+            ],
+            scratch_shapes=[pltpu.VMEM((chunks, width, width), f32)],
+        ),
+        out_shape=[
+            sds((count, part, width), bf16),
+            sds((count, part, width), f32),
+            sds((count, part, width), bf16),
+            sds((count, part, hidden_width), bf16),
+            sds((2, chunks // 2, width, width), bf16),
+            sds((8, width), f32),
+        ],
+        name="forward",
+        **kernel_params(2 * count * part * width * (width + 3 * hidden_width), 45e6, 4.7e6),
+    )(side_arr, tokens, attended, attended_recv, w_out, w_up, w_down, cotangent, pack)
+
+    gdown = gdown.reshape(2, hidden_width // 2, width)
+    gdown_recv = partner(gdown[1])
+    gdown_sum = (gdown[0].astype(f32) + gdown_recv.astype(f32)).astype(bf16)
+    gdown_sum = gdown_sum.reshape(lines, planes, chunks * share, width).transpose(1, 0, 2, 3)
+    grad_down = sum_rows(gdown_sum)
+
+    gmid, glow, gup, gup_bias, gnorm_two = pl.pallas_call(
+        backward_kernel,
+        grid_spec=pltpu.PrefetchScalarGridSpec(
+            num_scalar_prefetch=1,
+            grid=(count,),
+            in_specs=[
+                row_block(part, width),
+                row_block(part, hidden_width),
+                const(width, hidden_width),
+                const(hidden_width, width),
+                row_block(part, width),
+                row_block(part, width),
+                const(16, width),
+            ],
+            out_specs=[
+                row_block(part, width),
+                row_block(part, width),
+                const(2, chunks, wide, width),
+                const(chunks, 1, width),
+                const(8, width),
+            ],
+            scratch_shapes=[pltpu.VMEM((chunks, width, width), f32)],
+        ),
+        out_shape=[
+            sds((count, part, width), f32),
+            sds((count, part, width), bf16),
+            sds((2, chunks, wide, width), bf16),
+            sds((chunks, 1, width), f32),
+            sds((8, width), f32),
+        ],
+        name="backward",
+        **kernel_params(2 * count * part * width * 3 * hidden_width, 45e6),
+    )(side_arr, cotangent, slope, w_up, w_down, normed_two, middle, pack)
+
+    glow_other = partner(glow)
+    gup_recv = partner(gup[1])
+    gup_sum = (gup[0].astype(f32) + gup_recv.astype(f32)).astype(bf16)
+    gup_sum = gup_sum.reshape(chunks, lines, planes, share, width).transpose(2, 1, 0, 3, 4)
+    grad_up = sum_rows(gup_sum)
+    grad_up = grad_up.transpose(1, 0, 2).reshape(share, hidden_width)
+
+    gmixed, gout, gmixed_bias = pl.pallas_call(
+        attend_back_kernel,
+        grid_spec=pltpu.PrefetchScalarGridSpec(
+            num_scalar_prefetch=1,
+            grid=(count,),
+            in_specs=[
+                both_block(3 * wide),
+                both_block(wide),
+                both_block(wide),
+                row_block(part, width),
+                row_block(part, width),
+                const(wide, width),
+                row_block(length, 128),
+                row_block(length, 128),
+            ],
+            out_specs=[both_block(3 * wide), const(wide, width), const(8, 3 * wide)],
+            scratch_shapes=[pltpu.VMEM((heads, length, 128), bf16)] * 4
+            + [pltpu.VMEM((heads // 2, length // TQ_B, 2 * TQ_B, 128), bf16)] * 2
+            + [
+                pltpu.VMEM((length // TK_B, wide, TK_B), bf16),
+                pltpu.VMEM((length // TQ_B, wide, TQ_B), f32),
+                pltpu.VMEM((heads // 2, length, 128), f32),
+                pltpu.VMEM((heads // 2, length, 128), f32),
+                pltpu.VMEM((wide, width), f32),
+            ],
+        ),
+        out_shape=[
+            sds((2, count, part, 3 * wide), bf16),
+            sds((wide, width), bf16),
+            sds((8, 3 * wide), f32),
+        ],
+        name="attend_back",
+        **kernel_params(50e9, 30e6, 12e6),
+    )(flags_b, mixed, lse, attended, glow, glow_other, wo_mine, qx, kx)
+
+    tall = 2 * count * part
+    gqkv = lax.dot_general(
+        normed.reshape(tall, width),
+        gmixed.reshape(tall, 3 * wide),
+        (((0,), (0,)), ((), ())),
+        preferred_element_type=f32,
+    ).astype(bf16)
+    give_back = lax.dot_general(
+        gmixed[1].reshape(count * part, 3 * wide), w_qkv, NT, preferred_element_type=f32
+    ).astype(bf16)
+    recv_back = partner(give_back.reshape(count, part, width))
+
+    grad_input, gnorm_one = pl.pallas_call(
+        input_kernel,
+        grid=(count,),
+        in_specs=[
+            own_block(3 * wide),
+            const(width, 3 * wide),
+            row_block(part, width),
+            row_block(part, width),
+            row_block(part, width),
+            const(16, width),
+        ],
+        out_specs=[row_block(part, width), const(8, width)],
+        out_shape=[sds((count, part, width), f32), sds((8, width), f32)],
+        name="input_grad",
+        **kernel_params(2 * count * part * width * 3 * wide, 25e6),
+    )(gmixed, w_qkv, recv_back, tokens, gmid, pack)
+
+    spots_of = lambda vec: vec.reshape(2, lines, planes, 1, share)
+    zeros = jnp.zeros((wide,), f32)
+    place_half = lambda vec: jnp.concatenate([jnp.where(first, vec, zeros), jnp.where(first, zeros, vec)])
+    gqv = jnp.concatenate([place_half(gmixed_bias[0, :wide]), place_half(gmixed_bias[0, 2 * wide :])])
+    gup_vec = gup_bias.reshape(hidden_width)
+    gsmall = jnp.concatenate(
+        [
+            spots_of(gnorm_one[0]),
+            spots_of(gnorm_one[1]),
+            spots_of(gnorm_two[2]),
+            spots_of(gnorm_two[0]),
+            spots_of(gnorm_two[1]),
+            spots_of(gdown_bias[0]),
+            gqv.reshape(2, lines, planes, 2, share),
+            gup_vec.reshape(2, lines, planes, chunks, share),
+        ],
+        axis=3,
+    )
+    gsmall = jnp.pad(jnp.swapaxes(gsmall, 3, 4), ((0, 0),) * 4 + ((0, 128 - small_rows),)).astype(bf16)
+    gout = gout.reshape(lines, planes, share, 2, wide).transpose(3, 0, 1, 2, 4)
+    last = jnp.concatenate([gqkv.reshape(2, lines, planes, share, 3 * wide), gsmall, gout], axis=4)
+    last = sum_rows(last.transpose(2, 1, 0, 3, 4))
+    keep = lax.dynamic_index_in_dim(last, side, 0, keepdims=False)
+    pass_on = lax.dynamic_index_in_dim(last, 1 - side, 0, keepdims=False)
+    got = partner(pass_on[:, : 3 * wide + 128])
+    mine_q = keep[:, : 3 * wide].reshape(share, 3, 1, wide)
+    other_q = got[:, : 3 * wide].reshape(share, 3, 1, wide)
+    grad_qkv = jnp.where(
+        first, jnp.concatenate([mine_q, other_q], axis=2), jnp.concatenate([other_q, mine_q], axis=2)
+    ).reshape(share, 6 * wide)
+    vecs = (keep[:, 3 * wide : 3 * wide + small_rows] + got[:, 3 * wide : 3 * wide + small_rows]).T
+    both = last[:, :, 3 * wide + 128 :]
+    halves = lax.dynamic_index_in_dim(both, 0, 0, keepdims=False), lax.dynamic_index_in_dim(both, 1, 0, keepdims=False)
+    grad_out = jnp.concatenate(halves, axis=1)
+
+    new_qkv = 0.9 * avg_qkv + 0.1 * qkv_weight.astype(f32)
+    new_out = 0.9 * avg_out + 0.1 * out_weight.astype(f32)
+    new_up = 0.9 * avg_up + 0.1 * up_weight.astype(f32)
+    new_down = 0.9 * avg_down + 0.1 * down_weight.astype(f32)
+    return (
+        out_tokens,
+        grad_input,
+        vecs[0],
+        vecs[1],
+        grad_qkv,
+        vecs[6:8].reshape(2 * share),
+        grad_out,
+        vecs[2],
+        vecs[3],
+        vecs[4],
+        grad_up,
+        vecs[8 : 8 + chunks].reshape(chunks * share),
+        grad_down,
+        vecs[5],
+        new_qkv,
+        new_out,
+        new_up,
+        new_down,
+    )
+
+
+def specs_for(rows):
+    flat = ("seq",) + (rows if isinstance(rows, tuple) else (rows,))
+    grid, ids, vec, mat = P(rows, "seq", None), P(rows, "seq"), P(flat), P(flat, None)
+    ins = (grid, ids, grid, vec, vec, mat, vec, mat, vec, vec, vec, mat, vec, mat, vec, mat, mat, mat, mat)
+    outs = (grid, grid, vec, vec, mat, vec, mat, vec, vec, vec, mat, vec, mat, vec, mat, mat, mat, mat)
+    return ins, outs
+
+
 def solution(mesh):
-    placed = (
-        P("rows", "seq", None),
-        P("rows", "seq"),
-        P("rows", "seq", None),
-        P(("seq", "rows")),
-        P(("seq", "rows")),
-        P(("seq", "rows"), None),
-        P(("seq", "rows")),
-        P(("seq", "rows"), None),
-        P(("seq", "rows")),
-        P(("seq", "rows")),
-        P(("seq", "rows")),
-        P(("seq", "rows"), None),
-        P(("seq", "rows")),
-        P(("seq", "rows"), None),
-        P(("seq", "rows")),
-        P(("seq", "rows"), None),
-        P(("seq", "rows"), None),
-        P(("seq", "rows"), None),
-        P(("seq", "rows"), None),
-    )
+    parts, rows = mesh.shape["seq"], mesh.shape["rows"]
+    planes = 4
+    if parts != 2 or rows % planes:
+        ins, outs = specs_for("rows")
+        return jax.shard_map(on_device, mesh=mesh, in_specs=ins, out_specs=outs, check_vma=False)
+    lines = rows // planes
+    finer = Mesh(mesh.devices.reshape(parts, lines, 2, 2), ("seq", "line", "y", "x"))
+    ins, outs = specs_for(("line", "y", "x"))
     return jax.shard_map(
-        on_device,
-        mesh=mesh,
-        in_specs=placed,
-        out_specs=(
-            P("rows", "seq", None),
-            P("rows", "seq", None),
-            P(("seq", "rows")),
-            P(("seq", "rows")),
-            P(("seq", "rows"), None),
-            P(("seq", "rows")),
-            P(("seq", "rows"), None),
-            P(("seq", "rows")),
-            P(("seq", "rows")),
-            P(("seq", "rows")),
-            P(("seq", "rows"), None),
-            P(("seq", "rows")),
-            P(("seq", "rows"), None),
-            P(("seq", "rows")),
-            P(("seq", "rows"), None),
-            P(("seq", "rows"), None),
-            P(("seq", "rows"), None),
-            P(("seq", "rows"), None),
-        ),
-        check_vma=False,
-    )
+        functools.partial(pair_device, lines, planes), mesh=finer, in_specs=ins, out_specs=outs, check_vma=False
+    )

time: 932 us -> 552 us (0.59)
  matrix products: 454 us -> 15.7 us
  Pallas kernels: 0 us -> 243 us
  blocking collectives: 88.3 us -> 0 us
  starting transfers between devices: 0.83 us -> 68.1 us
  waiting for transfers between devices: 176 us -> 120 us
  local copies, waits for them, and re-layouts: 119 us -> 64.8 us
  other arithmetic: 68.1 us -> 32.7 us
  between operations: 15.3 us -> 1.68 us
    dot_general x26 -> x2, matrix products: 454 us -> 15.7 us  [the longest x1 11.2 us: pair_device(): lax.dot_general(normed.reshape(tall, width), gmixed.reshape(tall, 3 * wid...]
    pallas_call x0 -> x6, Pallas kernels: none -> 243 us  [the longest x1 99.8 us: pair_device(): pl.pallas_call(attend_back_kernel, grid_spec=pltpu.PrefetchScalarGridSpec...]
    reduce_scatter x4 -> x0, waiting for transfers between devices: 144 us -> none  [the longest x1 125 us: on_device(): lax.psum_scatter(grad_wqkv, ('seq', 'rows'), scatter_dimension=0, tiled=T...]
    unnamed x2 -> x0, blocking collectives: 84.3 us -> none
    all_to_all x0 -> x9, waiting for transfers between devices: none -> 78.9 us  [exchange(): return lax.all_to_all(value, axis, 0, 0, tiled=True)]
    unnamed x169 -> x52, local copies, waits for them, and re-layouts: 78.2 us -> 4.81 us
    all_to_all x0 -> x9, starting transfers between devices: none -> 58.3 us  [exchange(): return lax.all_to_all(value, axis, 0, 0, tiled=True)]
    ppermute x0 -> x21, waiting for transfers between devices: none -> 41.2 us  [the longest x8 40.6 us: flip(): return lax.ppermute(value, axis, [(0, 1), (1, 0)])]
  transfers between devices with their start and end apart: 12 -> 30, of which waited for: 5 -> 11; matrix products, arithmetic and copies ran while one was open for 65% -> 17% of each run, Pallas kernels for 0% -> 35%
where the time goes in v1:
time: 552 us; the launch traced here: 546 us
  Pallas kernels  243 us (44%)
  waiting for transfers between devices  120 us (22%)
  starting transfers between devices  68.1 us (12%)
  local copies, waits for them, and re-layouts  64.8 us (12%)
  other arithmetic  32.7 us (6%)
  matrix products  15.7 us (3%)
    pallas_call x1, Pallas kernels, pair_device(): pl.pallas_call(attend_back_kernel, grid_spec=pltpu.PrefetchScalarGridSpec...  99.8 us
    all_to_all x9, waiting for transfers between devices, exchange(): return lax.all_to_all(value, axis, 0, 0, tiled=True)  78.9 us
    all_to_all x9, starting transfers between devices, exchange(): return lax.all_to_all(value, axis, 0, 0, tiled=True)  58.3 us
    pallas_call x1, Pallas kernels, pair_device(): pl.pallas_call(forward_kernel, grid_spec=pltpu.PrefetchScalarGridSpec(num...  50.2 us
    ppermute x8, waiting for transfers between devices, flip(): return lax.ppermute(value, axis, [(0, 1), (1, 0)])  40.6 us
    pallas_call x1, Pallas kernels, pair_device(): pl.pallas_call(backward_kernel, grid_spec=pltpu.PrefetchScalarGridSpec(nu...  36.1 us
    pallas_call x1, Pallas kernels, pair_device(): pl.pallas_call(attend_kernel, grid_spec=pltpu.PrefetchScalarGridSpec(num_...  33.7 us
    pallas_call x1, Pallas kernels, pair_device(): pl.pallas_call(project_kernel, grid=(2, count), in_specs=[pl.BlockSpec((1...  13 us
  transfers between devices with their start and end apart: 30, of which 11 were waited for; matrix products, arithmetic and copies ran while one was open for 17% of the time, Pallas kernels for 35%

profile of v1, /device:TPU:0, one launch (start us, length us, event | category | flops | bytes accessed | tf_op | source)
XLA Modules:
  0.0 546.3 jit_solution(6866171196766476108)
XLA Ops:
  0.7 0.9 reshape.524
  10.5 1.6 pad_maximum_fusion
  13.0 6.1 %all-to-all-start = ((bf16[4,2,24,1280]{3,2,1,0:T(8,128)(2,1)}), bf16[4,2,24,1280]{3,2,1,0:T(8,128)(2,1)S(1)}, u32[]{:S(2)}, u32[]{:S(2)}) async-start(bf16[4,2,24,1280]{3,2,1,0:T(8,128)(2,1)} %broadcast_in_dim.148), calls=%async_computation | async-start | bytes 983040 | tf_op jit(solution)/shard_map/all_to_all | solution.py:615
  19.2 4.7 select_convert_fusion
  23.8 9.6 %all-to-all-done = bf16[4,2,24,1280]{3,2,1,0:T(8,128)(2,1)S(1)} async-done(((bf16[4,2,24,1280]{3,2,1,0:T(8,128)(2,1)}), bf16[4,2,24,1280]{3,2,1,0:T(8,128)(2,1)S(1)}, u32[]{:S(2)}, u32[]{:S(2)}) %all-to-all-start) | async-done | bytes 491552 | tf_op jit(solution)/shard_map/all_to_all | solution.py:615
  33.6 1.6 collective-permute-start.3
  35.4 1.6 collective-permute-start.5
  38.6 3.5 all-to-all-start.1
  42.8 1.4 collective-permute-start.6
  44.3 9.8 %collective-permute-done.4 = bf16[2,4,24,1280]{3,2,1,0:T(8,128)(2,1)S(1)} collective-permute-done((bf16[2,4,24,1280]{3,2,1,0:T(8,128)(2,1)S(1)}, bf16[2,4,24,1280]{3,2,1,0:T(8,128)(2,1)S(1)}, u32[]{:S(2)}, u32[]{:S(2)}) %collective-permute-start.4) | collective-permute-done | bytes 491552 | tf_op jit(solution)/shard_map/ppermute | solution.py:623
  54.6 2.5 all-to-all-done.1
  57.7 0.9 slice.212
  58.6 0.9 slice.211
  59.5 1.3 slice.203
  60.9 1.3 copy.332
  63.0 1.2 copy.331
  64.3 1.4 slice_reduce_fusion
  66.4 1.3 concatenate.114.pack_ref
  67.6 1.0 broadcast_in_dim.161
  68.6 4.0 all-to-all-start.2
  72.6 1.1 maximum_select_fusion.1
  74.4 13.0 %project.1 = (bf16[2,3,512,768]{3,2,1,0:T(8,128)(2,1)}, bf16[2,3,512,1152]{3,2,1,0:T(8,128)(2,1)}) custom-call(bf16[3,512,768]{2,1,0:T(8,128)(2,1)} %x_ref.3, bf16[3,512,768]{2,1,0:T(8,128)(2,1)} %collective-permute-done.1.other_ref, bf16[768,1152]{1,0:T(8,128)(2,1)} %bitcast.176, f32[16,768]{1,0:T(8,128)} %concatenate.114.pack_ref, ...), custom_call_target="tpu_custom_call" | custom-call | flops 5435817984 | bytes 20000000 | tf_op jit(solution)/shard_map/project/pallas_call | solution.py:767
  87.4 3.4 all-to-all-done.2
  91.3 33.7 %attend.1 = (bf16[2,3,512,384]{3,2,1,0:T(8,128)(2,1)}, f32[2,3,512,384]{3,2,1,0:T(8,128)}) custom-call(s32[3,16]{1,0:T(4,128)} %reshape.546.flag_ref, bf16[2,3,512,1152]{3,2,1,0:T(8,128)(2,1)} %get-tuple-element.42.mixed_ref, bf16[3,1024,128]{2,1,0:T(8,128)(2,1)} %get-tuple-element.110.qx_ref, bf16[3,1024,128]{2,1,0:T(8,128)(2,1)} %get-tuple-element.109.kx_ref), custom_call_target="tpu_custom_call" | custom-call | flops 16000000000 | bytes 20000000 | tf_op jit(solution)/shard_map/attend/pallas_call | solution.py:788
  125.0 1.4 slice_bitcast_fusion.5
  127.8 1.4 bitcast_dynamic-update-slice_fusion.2
  129.2 1.4 bitcast_dynamic-update-slice_fusion.1
  130.9 30.6 %collective-permute-done.9 = bf16[2,4,120,768]{3,2,0,1:T(8,128)(2,1)S(1)} collective-permute-done((bf16[2,4,120,768]{3,2,0,1:T(8,128)(2,1)S(1)}, bf16[2,4,120,768]{3,2,0,1:T(8,128)(2,1)S(1)}, u32[]{:S(2)}, u32[]{:S(2)}) %collective-permute-start.9) | collective-permute-done | bytes 1474592 | tf_op jit(solution)/shard_map/ppermute | solution.py:623
  161.8 3.1 broadcast_in_dim.170
  165.2 1.1 fusion.16
  166.4 1.1 fusion.15
  167.5 1.2 fusion.14
  168.7 1.0 copy-done.23
  169.7 50.2 %forward.1 = (bf16[3,512,768]{2,1,0:T(8,128)(2,1)}, f32[3,512,768]{2,1,0:T(8,128)}, bf16[3,512,768]{2,1,0:T(8,128)(2,1)}, bf16[3,512,3072]{2,1,0:T(8,128)(2,1)},...) custom-call(s32[1]{0:T(128)} %bitcast.side_ref, bf16[3,512,768]{2,1,0:T(8,128)(2,1)} %x_ref.3, ...), custom_call_target="tpu_custom_call" | custom-call | flops 23555211264 | bytes 45000000 | tf_op jit(solution)/shard_map/forward/pallas_call | solution.py:805
  220.0 4.1 fusion.50
  224.7 36.1 %backward.1 = (f32[3,512,768]{2,1,0:T(8,128)}, bf16[3,512,768]{2,1,0:T(8,128)(2,1)}, bf16[2,4,384,768]{3,2,1,0:T(8,128)(2,1)}, f32[4,1,768]{2,1,0:T(1,128)}, f32[8,768]{1,0:T(8,128)}) custom-call(s32[1]{0:T(128)} %bitcast.side_ref, bf16[3,512,768]{2,1,0:T(8,128)(2,1)} %grad_ref.3, bf16[3,512,3072]{2,1,0:T(8,128)(2,1)} %get-tuple-element.50.slope_ref, ...), custom_call_target="tpu_custom_call" | custom-call | flops 21743271936 | bytes 45000000 | tf_op jit(solution)/shard_map/backward/pallas_call | solution.py:848
  261.9 3.3 slice_bitcast_fusion
  270.2 2.3 fusion.2
  272.5 1.5 copy.360
  274.0 4.0 all-to-all-start.7
  278.1 99.8 %attend_back.1 = (bf16[2,3,512,1152]{3,2,1,0:T(8,128)(2,1)}, bf16[384,768]{1,0:T(8,128)(2,1)}, f32[8,1152]{1,0:T(8,128)}) custom-call(s32[3,32]{1,0:T(4,128)} %reshape.547.flag_ref, bf16[2,3,512,1152]{3,2,1,0:T(8,128)(2,1)} %get-tuple-element.42.mixed_ref, f32[2,3,512,384]{3,2,1,0:T(8,128)} %get-tuple-element.49.lse_ref, ...), custom_call_target="tpu_custom_call" | custom-call | flops 49999998976 | bytes 30000000 | tf_op jit(solution)/shard_map/attend_back/pallas_call | solution.py:889
  377.9 2.4 slice.175
  380.4 4.5 convolution_convert_fusion
  386.5 2.9 fusion.3
  389.4 1.7 copy.378
  391.9 1.4 copy-done.1
  393.3 4.9 all-to-all-start.5
  398.5 11.2 %fusion.4 = bf16[768,1152]{1,0:T(8,128)(2,1)} fusion(bf16[2,3,512,768]{3,2,1,0:T(8,128)(2,1)} %get-tuple-element.57, bf16[2,3,512,1152]{3,2,1,0:T(8,128)(2,1)} %get-tuple-element.54.gmixed_ref), kind=kOutput, calls=%fused_computation.9 | convolution fusion | flops 5436702720 | bytes 13565952 | tf_op jit(solution)/shard_map/dot_general | solution.py:925
  409.7 3.0 reduce_sum.67
  412.8 14.6 %all-to-all-done.5 = bf16[4,4,4,24,768]{4,3,1,2,0:T(8,128)(2,1)S(1)} async-done(((bf16[4,4,4,24,768]{4,3,1,2,0:T(8,128)(2,1)}), bf16[4,4,4,24,768]{4,3,1,2,0:T(8,128)(2,1)S(1)}, u32[]{:S(2)}, u32[]{:S(2)}) %all-to-all-start.5) | async-done | bytes 2359328 | tf_op jit(solution)/shard_map/all_to_all | solution.py:615
  427.4 23.9 %all-to-all-start.8 = ((bf16[4,96,768]{2,1,0:T(8,128)(2,1)}), bf16[4,96,768]{2,1,0:T(8,128)(2,1)S(1)}, u32[]{:S(2)}, u32[]{:S(2)}) async-start(bf16[4,96,768]{2,1,0:T(8,128)(2,1)} %reduce_sum.67), calls=%async_computation.8 | async-start | bytes 1179648 | tf_op jit(solution)/shard_map/all_to_all | solution.py:615
  451.3 10.4 %input_grad.1 = (f32[3,512,768]{2,1,0:T(8,128)}, f32[8,768]{1,0:T(8,128)}) custom-call(bf16[2,3,512,1152]{3,2,1,0:T(8,128)(2,1)} %get-tuple-element.54.gmixed_ref, bf16[768,1152]{1,0:T(8,128)(2,1)} %bitcast.177, bf16[3,512,768]{2,1,0:T(8,128)(2,1)} %collective-permute-done.17.recv_ref, bf16[3,512,768]{2,1,0:T(8,128)(2,1)} %x_ref.3, ...), custom_call_target="tpu_custom_call" | custom-call | flops 2717908992 | bytes 25000000 | tf_op jit(solution)/shard_map/input_grad/pallas_call | solution.py:936
  462.7 1.7 concatenate.124
  464.7 2.7 fusion.7
  468.3 3.6 all-to-all-start.3
  472.0 1.7 multiply_add_fusion
  473.7 2.1 reduce_sum.65
  476.7 24.6 %all-to-all-done.3 = bf16[4,4,2,24,1664]{4,3,1,2,0:T(8,128)(2,1)S(1)} async-done(((bf16[4,4,2,24,1664]{4,3,1,2,0:T(8,128)(2,1)}), bf16[4,4,2,24,1664]{4,3,1,2,0:T(8,128)(2,1)S(1)}, u32[]{:S(2)}, u32[]{:S(2)}) %all-to-all-start.3) | async-done | bytes 2555936 | tf_op jit(solution)/shard_map/all_to_all | solution.py:615
  501.3 4.8 all-to-all-start.6
  506.7 1.7 multiply_add_fusion.1
  510.0 11.2 %all-to-all-done.6 = bf16[4,4,24,768]{3,2,1,0:T(8,128)(2,1)} async-done(((bf16[4,4,24,768]{3,2,1,0:T(8,128)(2,1)}), bf16[4,4,24,768]{3,2,1,0:T(8,128)(2,1)}, u32[]{:S(2)}, u32[]{:S(2)}) %all-to-all-start.6) | async-done | bytes 589856 | tf_op jit(solution)/shard_map/all_to_all | solution.py:615
  521.2 3.5 all-to-all-start.4
  525.5 1.2 convert_reduce_fusion.2
  528.2 13.0 %all-to-all-done.4 = bf16[4,2,24,1664]{3,2,1,0:T(8,128)(2,1)S(1)} async-done(((bf16[4,2,24,1664]{3,2,1,0:T(8,128)(2,1)}), bf16[4,2,24,1664]{3,2,1,0:T(8,128)(2,1)S(1)}, u32[]{:S(2)}, u32[]{:S(2)}) %all-to-all-start.4) | async-done | bytes 639008 | tf_op jit(solution)/shard_map/all_to_all | solution.py:615
  (213 shorter events, 40.4 us)
Async XLA Ops:
  0.7 18.4 %copy-start.16 = (s32[3,512]{1,0:T(4,128)S(1)}, s32[3,512]{1,0:T(4,128)}, u32[]{:S(2)}) copy-start(s32[3,512]{1,0:T(4,128)} %param.20) | copy-start | bytes 18436
  8.6 3.5 collective-permute-start.2
  9.2 65.2 %collective-permute-start.1 = (bf16[3,512,768]{2,1,0:T(8,128)(2,1)}, bf16[3,512,768]{2,1,0:T(8,128)(2,1)}, u32[]{:S(2)}, u32[]{:S(2)}) collective-permute-start(bf16[3,512,768]{2,1,0:T(8,128)(2,1)} %x_ref.3), channel_id=1, source_target_pairs={{0,16},{16,0},{1,17},{17,1},{2,18},{18,2},{3,19},{19,3},{4,20},{20... | collective-permute-start | bytes 7077896 | tf_op jit(solution)/shard_map/ppermute | solution.py:611
  9.2 9.9 %collective-permute-start = (s32[3,512]{1,0:T(4,128)}, s32[3,512]{1,0:T(4,128)S(1)}, u32[]{:S(2)}, u32[]{:S(2)}) collective-permute-start(s32[3,512]{1,0:T(4,128)} %param.20), channel_id=1, source_target_pairs={{0,16},{16,0},{1,17},{17,1},{2,18},{18,2},{3,19},{19,3},{4,20},{20... | collective-permute-start | bytes 18440 | tf_op jit(solution)/shard_map/ppermute | solution.py:611
  13.0 24.7 %copy-start.11 = (bf16[24,3072]{1,0:T(8,128)(2,1)S(1)}, bf16[24,3072]{1,0:T(8,128)(2,1)}, u32[]{:S(2)}) copy-start(bf16[24,3072]{1,0:T(8,128)(2,1)} %param.30) | copy-start | bytes 442372
  13.0 20.5 %all-to-all-start = ((bf16[4,2,24,1280]{3,2,1,0:T(8,128)(2,1)}), bf16[4,2,24,1280]{3,2,1,0:T(8,128)(2,1)S(1)}, u32[]{:S(2)}, u32[]{:S(2)}) async-start(bf16[4,2,24,1280]{3,2,1,0:T(8,128)(2,1)} %broadcast_in_dim.148), calls=%async_computation | async-start | bytes 983040 | tf_op jit(solution)/shard_map/all_to_all | solution.py:615
  33.6 8.5 %collective-permute-start.3 = (bf16[4,24,1280]{2,1,0:T(8,128)(2,1)S(1)}, bf16[4,24,1280]{2,1,0:T(8,128)(2,1)S(1)}, u32[]{:S(2)}, u32[]{:S(2)}) collective-permute-start(bf16[4,24,1280]{2,1,0:T(8,128)(2,1)S(1)} %get-tuple-element.100), channel_id=1, source_target_pairs={{0,1},{1,0},{2,3},{3,2},{4,5},{5,4},{6,7},{7,6},{8,9},{9,8},{10,11... | collective-permute-start | bytes 737288 | tf_op jit(solution)/shard_map/ppermute | solution.py:623
  35.3 8.9 %copy-start.18 = (s32[3,4]{1,0:T(4,128)}, s32[3,4]{1,0:T(4,128)S(1)}, u32[]{:S(2)}) copy-start(s32[3,4]{1,0:T(4,128)S(1)} %get-tuple-element.80) | copy-start | bytes 148
  35.4 8.9 %copy-start.20 = (s32[3,4]{1,0:T(4,128)}, s32[3,4]{1,0:T(4,128)S(1)}, u32[]{:S(2)}) copy-start(s32[3,4]{1,0:T(4,128)S(1)} %get-tuple-element.81) | copy-start | bytes 148
  35.4 7.3 %collective-permute-start.5 = (bf16[4,24,1280]{2,1,0:T(8,128)(2,1)S(1)}, bf16[4,24,1280]{2,1,0:T(8,128)(2,1)S(1)}, u32[]{:S(2)}, u32[]{:S(2)}) collective-permute-start(bf16[4,24,1280]{2,1,0:T(8,128)(2,1)S(1)} %get-tuple-element.102), channel_id=1, source_target_pairs={{0,2},{2,0},{1,3},{3,1},{4,6},{6,4},{5,7},{7,5},{8,10},{10,8},{9,1... | collective-permute-start | bytes 737288 | tf_op jit(solution)/shard_map/ppermute | solution.py:623
  38.6 18.6 %all-to-all-start.1 = ((bf16[4,24,3072]{2,1,0:T(8,128)(2,1)}), bf16[4,24,3072]{2,1,0:T(8,128)(2,1)S(1)}, u32[]{:S(2)}, u32[]{:S(2)}) async-start(bf16[4,24,3072]{2,1,0:T(8,128)(2,1)} %broadcast_in_dim.160), calls=%async_computation.1 | async-start | bytes 1179648 | tf_op jit(solution)/shard_map/all_to_all | solution.py:615
  42.1 12.0 %collective-permute-start.4 = (bf16[2,4,24,1280]{3,2,1,0:T(8,128)(2,1)S(1)}, bf16[2,4,24,1280]{3,2,1,0:T(8,128)(2,1)S(1)}, u32[]{:S(2)}, u32[]{:S(2)}) collective-permute-start(bf16[2,4,24,1280]{3,2,1,0:T(8,128)(2,1)S(1)} %maximum_select_fusion.5), channel_id=1, source_target_pairs={{0,2},{2,0},{1,3},{3,1},{4,6},{6,4},{5,7},{7,5},{8,10},{10,8},{9,1... | collective-permute-start | bytes 1474568 | tf_op jit(solution)/shard_map/ppermute | solution.py:623
  42.8 11.7 %collective-permute-start.6 = (bf16[2,4,24,1280]{3,2,1,0:T(8,128)(2,1)S(1)}, bf16[2,4,24,1280]{3,2,1,0:T(8,128)(2,1)S(1)}, u32[]{:S(2)}, u32[]{:S(2)}) collective-permute-start(bf16[2,4,24,1280]{3,2,1,0:T(8,128)(2,1)S(1)} %maximum_select_fusion.7), channel_id=1, source_target_pairs={{0,1},{1,0},{2,3},{3,2},{4,5},{5,4},{6,7},{7,6},{8,9},{9,8},{10,11... | collective-permute-start | bytes 1474568 | tf_op jit(solution)/shard_map/ppermute | solution.py:623
  57.1 15.5 %collective-permute-start.12 = (bf16[4,24,3072]{2,1,0:T(8,128)(2,1)S(1)}, bf16[4,24,3072]{2,1,0:T(8,128)(2,1)S(1)}, u32[]{:S(2)}, u32[]{:S(2)}) collective-permute-start(bf16[4,24,3072]{2,1,0:T(8,128)(2,1)S(1)} %all-to-all-done.1), channel_id=1, source_target_pairs={{0,1},{1,0},{2,3},{3,2},{4,5},{5,4},{6,7},{7,6},{8,9},{9,8},{10,11... | collective-permute-start | bytes 1769480 | tf_op jit(solution)/shard_map/ppermute | solution.py:623
  60.9 6.8 %copy-start.8 = (bf16[120,768]{1,0:T(8,128)(2,1)S(1)}, bf16[120,768]{1,0:T(8,128)(2,1)}, u32[]{:S(2)}) copy-start(bf16[120,768]{1,0:T(8,128)(2,1)} %pad_maximum_fusion) | copy-start | bytes 552964
  68.6 22.2 %all-to-all-start.2 = ((bf16[4,120,768]{2,1,0:T(8,128)(2,1)}), bf16[4,120,768]{2,1,0:T(8,128)(2,1)S(1)}, u32[]{:S(2)}, u32[]{:S(2)}) async-start(bf16[4,120,768]{2,1,0:T(8,128)(2,1)} %broadcast_in_dim.161), calls=%async_computation.2 | async-start | bytes 1474560 | tf_op jit(solution)/shard_map/all_to_all | solution.py:615
  73.7 52.7 %collective-permute-start.13 = (bf16[2,4,24,3072]{3,2,0,1:T(8,128)(2,1)}, bf16[2,4,24,3072]{3,2,0,1:T(8,128)(2,1)}, u32[]{:S(2)}, u32[]{:S(2)}) collective-permute-start(bf16[2,4,24,3072]{3,2,0,1:T(8,128)(2,1)} %maximum_select_fusion.1), channel_id=1, source_target_pairs={{0,2},{2,0},{1,3},{3,1},{4,6},{6,4},{5,7},{7,5},{8,10},{10,8},{9,1... | collective-permute-start | bytes 3538952 | tf_op jit(solution)/shard_map/ppermute | solution.py:623
  74.3 55.0 %collective-permute-start.14 = (bf16[2,4,24,3072]{3,2,0,1:T(8,128)(2,1)}, bf16[2,4,24,3072]{3,2,0,1:T(8,128)(2,1)}, u32[]{:S(2)}, u32[]{:S(2)}) collective-permute-start(bf16[2,4,24,3072]{3,2,0,1:T(8,128)(2,1)} %maximum_select_fusion.1), channel_id=1, source_target_pairs={{0,16},{16,0},{1,17},{17,1},{2,18},{18,2},{3,19},{19,3},{4,20},{20... | collective-permute-start | bytes 3538952 | tf_op jit(solution)/shard_map/ppermute | solution.py:611
  90.8 36.1 %collective-permute-start.8 = (bf16[4,120,768]{2,1,0:T(8,128)(2,1)S(1)}, bf16[4,120,768]{2,1,0:T(8,128)(2,1)S(1)}, u32[]{:S(2)}, u32[]{:S(2)}) collective-permute-start(bf16[4,120,768]{2,1,0:T(8,128)(2,1)S(1)} %all-to-all-done.2), channel_id=1, source_target_pairs={{0,2},{2,0},{1,3},{3,1},{4,6},{6,4},{5,7},{7,5},{8,10},{10,8},{9,1... | collective-permute-start | bytes 2211848 | tf_op jit(solution)/shard_map/ppermute | solution.py:623
  126.4 42.3 %collective-permute-start.7 = (bf16[3,512,384]{2,1,0:T(8,128)(2,1)S(1)}, bf16[3,512,384]{2,1,0:T(8,128)(2,1)S(1)}, u32[]{:S(2)}, u32[]{:S(2)}) collective-permute-start(bf16[3,512,384]{2,1,0:T(8,128)(2,1)S(1)} %slice_bitcast_fusion.5), channel_id=1, source_target_pairs={{0,16},{16,0},{1,17},{17,1},{2,18},{18,2},{3,19},{19,3},{4,20},{20... | collective-permute-start | bytes 3538952 | tf_op jit(solution)/shard_map/ppermute | solution.py:611
  126.5 35.0 %collective-permute-start.15 = (bf16[2,4,24,3072]{3,2,0,1:T(8,128)(2,1)}, bf16[2,4,24,3072]{3,2,0,1:T(8,128)(2,1)S(1)}, u32[]{:S(2)}, u32[]{:S(2)}) collective-permute-start(bf16[2,4,24,3072]{3,2,0,1:T(8,128)(2,1)} %collective-permute-done.13), channel_id=1, source_target_pairs={{0,16},{16,0},{1,17},{17,1},{2,18},{18,2},{3,19},{19,3},{4,20},{20... | collective-permute-start | bytes 3538952 | tf_op jit(solution)/shard_map/ppermute | solution.py:611
  127.1 34.3 %collective-permute-start.9 = (bf16[2,4,120,768]{3,2,0,1:T(8,128)(2,1)S(1)}, bf16[2,4,120,768]{3,2,0,1:T(8,128)(2,1)S(1)}, u32[]{:S(2)}, u32[]{:S(2)}) collective-permute-start(bf16[2,4,120,768]{3,2,0,1:T(8,128)(2,1)S(1)} %maximum_select_fusion), channel_id=1, source_target_pairs={{0,1},{1,0},{2,3},{3,2},{4,5},{5,4},{6,7},{7,6},{8,9},{9,8},{10,11... | collective-permute-start | bytes 4423688 | tf_op jit(solution)/shard_map/ppermute | solution.py:623
  130.6 31.1 %collective-permute-start.10 = (bf16[2,4,120,768]{3,2,0,1:T(8,128)(2,1)S(1)}, bf16[2,4,120,768]{3,2,0,1:T(8,128)(2,1)S(1)}, u32[]{:S(2)}, u32[]{:S(2)}) collective-permute-start(bf16[2,4,120,768]{3,2,0,1:T(8,128)(2,1)S(1)} %maximum_select_fusion), channel_id=1, source_target_pairs={{0,16},{16,0},{1,17},{17,1},{2,18},{18,2},{3,19},{19,3},{4,20},{20... | collective-permute-start | bytes 4423688 | tf_op jit(solution)/shard_map/ppermute | solution.py:611
  161.5 6.0 %collective-permute-start.11 = (bf16[2,4,120,768]{3,2,0,1:T(8,128)(2,1)S(1)}, bf16[2,4,120,768]{3,2,0,1:T(8,128)(2,1)S(1)}, u32[]{:S(2)}, u32[]{:S(2)}) collective-permute-start(bf16[2,4,120,768]{3,2,0,1:T(8,128)(2,1)S(1)} %collective-permute-done.9), channel_id=1, source_target_pairs={{0,16},{16,0},{1,17},{17,1},{2,18},{18,2},{3,19},{19,3},{4,20},{20... | collective-permute-start | bytes 4423688 | tf_op jit(solution)/shard_map/ppermute | solution.py:611
  161.6 3.6 copy-start.3
  167.5 2.2 copy-start.4
  168.7 1.0 copy-start.23
  224.0 46.2 %collective-permute-start.20 = (bf16[1536,768]{1,0:T(8,128)(2,1)}, bf16[1536,768]{1,0:T(8,128)(2,1)}, u32[]{:S(2)}, u32[]{:S(2)}) collective-permute-start(bf16[1536,768]{1,0:T(8,128)(2,1)} %bitcast.84), channel_id=1, source_target_pairs={{0,16},{16,0},{1,17},{17,1},{2,18},{18,2},{3,19},{19,3},{4,20},{20... | collective-permute-start | bytes 7077896 | tf_op jit(solution)/shard_map/ppermute | solution.py:611
  224.7 36.5 %copy-start.19 = (s32[3,4]{1,0:T(4,128)S(1)}, s32[3,4]{1,0:T(4,128)}, u32[]{:S(2)}) copy-start(s32[3,4]{1,0:T(4,128)} %copy-done.18) | copy-start | bytes 148
  224.7 36.5 %copy-start.21 = (s32[3,4]{1,0:T(4,128)S(1)}, s32[3,4]{1,0:T(4,128)}, u32[]{:S(2)}) copy-start(s32[3,4]{1,0:T(4,128)} %copy-done.20) | copy-start | bytes 148
  260.8 17.3 %collective-permute-start.16 = (bf16[3,512,768]{2,1,0:T(8,128)(2,1)}, bf16[3,512,768]{2,1,0:T(8,128)(2,1)}, u32[]{:S(2)}, u32[]{:S(2)}) collective-permute-start(bf16[3,512,768]{2,1,0:T(8,128)(2,1)} %get-tuple-element.53.own_ref), channel_id=1, source_target_pairs={{0,16},{16,0},{1,17},{17,1},{2,18},{18,2},{3,19},{19,3},{4,20},{20... | collective-permute-start | bytes 7077896 | tf_op jit(solution)/shard_map/ppermute | solution.py:611
  261.9 3.8 copy-start.22
  261.9 7.5 %copy-start.5 = (bf16[2,4,2,2,24,768]{5,4,3,2,1,0:T(8,128)(2,1)S(1)}, bf16[2,4,2,2,24,768]{5,4,3,2,1,0:T(8,128)(2,1)}, u32[]{:S(2)}) copy-start(bf16[2,4,2,2,24,768]{5,4,3,2,1,0:T(8,128)(2,1)} %copy-done.4) | copy-start | bytes 3538948
  265.2 121.2 %collective-permute-start.19 = (bf16[4,384,768]{2,1,0:T(8,128)(2,1)}, bf16[4,384,768]{2,1,0:T(8,128)(2,1)}, u32[]{:S(2)}, u32[]{:S(2)}) collective-permute-start(bf16[4,384,768]{2,1,0:T(8,128)(2,1)} %slice_bitcast_fusion), channel_id=1, source_target_pairs={{0,16},{16,0},{1,17},{17,1},{2,18},{18,2},{3,19},{19,3},{4,20},{20... | collective-permute-start | bytes 7077896 | tf_op jit(solution)/shard_map/ppermute | solution.py:611
  274.0 117.8 %all-to-all-start.7 = ((bf16[4,4,96,768]{3,2,1,0:T(8,128)(2,1)}), bf16[4,4,96,768]{3,2,1,0:T(8,128)(2,1)S(1)}, u32[]{:S(2)}, u32[]{:S(2)}) async-start(bf16[4,4,96,768]{3,2,1,0:T(8,128)(2,1)} %copy.360), calls=%async_computation.7 | async-start | bytes 4718592 | tf_op jit(solution)/shard_map/all_to_all | solution.py:615
  377.9 2.5 copy-start.2
  385.0 66.3 %collective-permute-start.17 = (bf16[3,512,768]{2,1,0:T(8,128)(2,1)}, bf16[3,512,768]{2,1,0:T(8,128)(2,1)}, u32[]{:S(2)}, u32[]{:S(2)}) collective-permute-start(bf16[3,512,768]{2,1,0:T(8,128)(2,1)} %bitcast.66), channel_id=1, source_target_pairs={{0,16},{16,0},{1,17},{17,1},{2,18},{18,2},{3,19},{19,3},{4,20},{20... | collective-permute-start | bytes 7077896 | tf_op jit(solution)/shard_map/ppermute | solution.py:611
  391.9 1.4 copy-start.1
  391.9 6.4 %copy-start.9 = (bf16[384,768]{1,0:T(8,128)(2,1)S(1)}, bf16[384,768]{1,0:T(8,128)(2,1)}, u32[]{:S(2)}) copy-start(bf16[384,768]{1,0:T(8,128)(2,1)} %get-tuple-element.63) | copy-start | bytes 1769476
  393.3 34.1 %all-to-all-start.5 = ((bf16[4,4,4,24,768]{4,3,1,2,0:T(8,128)(2,1)}), bf16[4,4,4,24,768]{4,3,1,2,0:T(8,128)(2,1)S(1)}, u32[]{:S(2)}, u32[]{:S(2)}) async-start(bf16[4,4,4,24,768]{4,3,1,2,0:T(8,128)(2,1)} %bitcast.175), calls=%async_computation.5 | async-start | bytes 4718592 | tf_op jit(solution)/shard_map/all_to_all | solution.py:615
  427.4 34.3 %copy-start = (bf16[4,4,4,24,768]{4,3,1,2,0:T(8,128)(2,1)}, bf16[4,4,4,24,768]{4,3,1,2,0:T(8,128)(2,1)S(1)}, u32[]{:S(2)}) copy-start(bf16[4,4,4,24,768]{4,3,1,2,0:T(8,128)(2,1)S(1)} %all-to-all-done.5) | copy-start | bytes 7077892
  427.4 40.1 %all-to-all-start.8 = ((bf16[4,96,768]{2,1,0:T(8,128)(2,1)}), bf16[4,96,768]{2,1,0:T(8,128)(2,1)S(1)}, u32[]{:S(2)}, u32[]{:S(2)}) async-start(bf16[4,96,768]{2,1,0:T(8,128)(2,1)} %reduce_sum.67), calls=%async_computation.8 | async-start | bytes 1179648 | tf_op jit(solution)/shard_map/all_to_all | solution.py:615
  467.4 4.5 copy-start.10
  467.5 0.8 copy-start.6
  468.3 33.0 %all-to-all-start.3 = ((bf16[4,4,2,24,1664]{4,3,1,2,0:T(8,128)(2,1)}), bf16[4,4,2,24,1664]{4,3,1,2,0:T(8,128)(2,1)S(1)}, u32[]{:S(2)}, u32[]{:S(2)}) async-start(bf16[4,4,2,24,1664]{4,3,1,2,0:T(8,128)(2,1)} %fusion.7), calls=%async_computation.3 | async-start | bytes 5111808 | tf_op jit(solution)/shard_map/all_to_all | solution.py:615
  473.7 32.4 %copy-start.15 = (bf16[24,768]{1,0:T(8,128)(2,1)S(1)}, bf16[24,768]{1,0:T(8,128)(2,1)}, u32[]{:S(2)}) copy-start(bf16[24,768]{1,0:T(8,128)(2,1)} %param.26) | copy-start | bytes 110596
  473.7 32.4 %copy-start.17 = (f32[24,768]{1,0:T(8,128)S(1)}, f32[24,768]{1,0:T(8,128)}, u32[]{:S(2)}) copy-start(f32[24,768]{1,0:T(8,128)} %param.35) | copy-start | bytes 221188
  473.7 33.0 %copy-start.12 = (bf16[24,3072]{1,0:T(8,128)(2,1)S(1)}, bf16[24,3072]{1,0:T(8,128)(2,1)}, u32[]{:S(2)}) copy-start(bf16[24,3072]{1,0:T(8,128)(2,1)} %param.30) | copy-start | bytes 442372
  501.3 20.0 %all-to-all-start.6 = ((bf16[4,4,24,768]{3,2,1,0:T(8,128)(2,1)}), bf16[4,4,24,768]{3,2,1,0:T(8,128)(2,1)}, u32[]{:S(2)}, u32[]{:S(2)}) async-start(bf16[4,4,24,768]{3,2,1,0:T(8,128)(2,1)} %copy.356), calls=%async_computation.6 | async-start | bytes 1179648 | tf_op jit(solution)/shard_map/all_to_all | solution.py:615
  508.4 16.3 %copy-start.13 = (bf16[24,2304]{1,0:T(8,128)(2,1)S(1)}, bf16[24,2304]{1,0:T(8,128)(2,1)}, u32[]{:S(2)}) copy-start(bf16[24,2304]{1,0:T(8,128)(2,1)} %param.24) | copy-start | bytes 331780
  508.4 16.3 %copy-start.14 = (f32[24,2304]{1,0:T(8,128)S(1)}, f32[24,2304]{1,0:T(8,128)}, u32[]{:S(2)}) copy-start(f32[24,2304]{1,0:T(8,128)} %param.34) | copy-start | bytes 663556
  509.2 18.2 %copy-start.7 = (bf16[4,96,768]{2,1,0:T(8,128)(2,1)S(1)}, bf16[4,96,768]{2,1,0:T(8,128)(2,1)}, u32[]{:S(2)}) copy-start(bf16[4,96,768]{2,1,0:T(8,128)(2,1)} %copy-done.6) | copy-start | bytes 1769476
  521.2 19.9 %all-to-all-start.4 = ((bf16[4,2,24,1664]{3,2,1,0:T(8,128)(2,1)}), bf16[4,2,24,1664]{3,2,1,0:T(8,128)(2,1)S(1)}, u32[]{:S(2)}, u32[]{:S(2)}) async-start(bf16[4,2,24,1664]{3,2,1,0:T(8,128)(2,1)} %copy.351), calls=%async_computation.4 | async-start | bytes 1277952 | tf_op jit(solution)/shard_map/all_to_all | solution.py:615
  541.3 1.4 collective-permute-start.18
